TPU v7x, 128 devices: a whole 4x4x4 slice. The times are simulated.
128 devices in a mesh: row: 4 (over x), col: 16 (over z, y_lo, core), depth: 2 (over y_hi).
Axes of the slice: x: 4, y: 4 (y_hi: 2, y_lo: 2; y = y_hi * 2 + y_lo), z: 4, core: 2. Of those that a mesh axis runs over, the one named last changes fastest.
Arguments:
- tokens: bfloat16 [1024, 7168], P(('col', 'depth'), 'row'), may hold values from -6 to 6
- first_weight: bfloat16 [7168, 28672], P('row', 'col'), may hold values from -0.0625 to 0.0625
- second_weight: bfloat16 [28672, 7168], P('col', 'row'), may hold values from -0.03125 to 0.03125
- upstream: bfloat16 [1024, 7168], P(('col', 'depth'), 'row'), may hold values from -6 to 6
Outputs:
- layer_out: bfloat16 [1024, 7168], P(('col', 'depth'), 'row')
- token_grad: bfloat16 [1024, 7168], P(('col', 'depth'), 'row')
- first_grad: float32 [7168, 28672], P(('row', 'depth'), 'col')
- second_grad: float32 [28672, 7168], P(('col', 'depth'), 'row')
All inputs are finite; a program needn't handle non-finite values.
Results may differ from a plain program's by a relative error of at most 0.005.
Values may be sent and summed in bfloat16 or wider, within the bound.
A program may use at most 192 MiB of HBM per device.

v0:
```python
import math

import jax
import jax.numpy as jnp
from jax import lax
from jax.sharding import PartitionSpec as P


def gelu_tanh(hidden):
    scale = math.sqrt(2.0 / math.pi)
    inner = scale * (hidden + 0.044715 * hidden * hidden * hidden)
    return 0.5 * hidden * (1.0 + jnp.tanh(inner))


def gelu_slope(hidden):
    scale = math.sqrt(2.0 / math.pi)
    inner = scale * (hidden + 0.044715 * hidden * hidden * hidden)
    tanh_val = jnp.tanh(inner)
    return 0.5 * (1.0 + tanh_val) + 0.5 * hidden * (1.0 - tanh_val * tanh_val) * scale * (
        1.0 + 3.0 * 0.044715 * hidden * hidden
    )


def contract_lead(left, right):
    return lax.dot_general(
        left, right, (((0,), (0,)), ((), ())), preferred_element_type=jnp.float32
    )


def contract_last(left, right):
    return lax.dot_general(
        left, right, (((1,), (1,)), ((), ())), preferred_element_type=jnp.float32
    )


def local(tokens, first_weight, second_weight, upstream):
    group = lax.all_gather(tokens, "col", axis=0, tiled=True)
    hidden = lax.psum(jnp.dot(group, first_weight, preferred_element_type=jnp.float32), "row")
    activ = gelu_tanh(hidden).astype(jnp.bfloat16)
    slope = gelu_slope(hidden)
    layer_out = lax.psum_scatter(
        jnp.dot(activ, second_weight, preferred_element_type=jnp.float32),
        "col",
        scatter_dimension=0,
        tiled=True,
    ).astype(jnp.bfloat16)
    back = lax.all_gather(upstream, "col", axis=0, tiled=True)
    back_hidden = lax.psum(contract_last(back, second_weight), "row")
    delta = (back_hidden * slope).astype(jnp.bfloat16)
    token_grad = lax.psum_scatter(
        contract_last(delta, first_weight), "col", scatter_dimension=0, tiled=True
    ).astype(jnp.bfloat16)
    first_grad = lax.psum_scatter(
        contract_lead(group, delta), "depth", scatter_dimension=0, tiled=True
    )
    second_grad = lax.psum_scatter(
        contract_lead(activ, back), "depth", scatter_dimension=0, tiled=True
    )
    return (layer_out, token_grad, first_grad, second_grad)


def solution(mesh):
    in_specs = (
        P(("col", "depth"), "row"),
        P("row", "col"),
        P("col", "row"),
        P(("col", "depth"), "row"),
    )
    out_specs = (
        P(("col", "depth"), "row"),
        P(("col", "depth"), "row"),
        P(("row", "depth"), "col"),
        P(("col", "depth"), "row"),
    )
    return jax.shard_map(local, mesh=mesh, in_specs=in_specs, out_specs=out_specs, check_vma=False)
```

profile of v0, /device:TPU:1, one launch (start us, length us, event | category | flops | bytes accessed | tf_op | source)
XLA Modules:
  0.0 698.7 jit_solution(15861303362281982270)
XLA Ops:
  7.2 0.0 all-gather.5.cloned.1.call-start
  7.2 0.7 all-gather.5.cloned.1.call-update
  7.9 0.0 all-gather.3.cloned.1.call-start
  7.9 0.7 all-gather.3.cloned.1.call-update
  8.6 0.0 all-reduce.3.cloned.1.call-start
  8.7 38.3 %all-gather.5.cloned.1.call-done = bf16[512,1792]{1,0:T(8,128)(2,1)} async-done(((bf16[32,1792]{1,0:T(8,128)(2,1)}), bf16[512,1792]{1,0:T(8,128)(2,1)}) %all-gather.5.cloned.1.call-update) | async-done | bytes 1835024 | tf_op jit(solution)/shard_map/all_gather | solution.py:47
  47.0 8.7 %fusion.10 = f32[512,1792]{1,0:T(8,128)} fusion(bf16[512,1792]{1,0:T(8,128)(2,1)} %all-gather.5.cloned.1.call-done, bf16[1792,1792]{1,0:T(8,128)(2,1)} %param.6), kind=kOutput, calls=%fused_computation.14 | convolution fusion | flops 3288334336 | bytes 11927552 | tf_op jit(solution)/shard_map/dot_general | solution.py:31
  55.8 26.6 %all-gather.3.cloned.1.call-done = bf16[512,1792]{1,0:T(8,128)(2,1)} async-done(((bf16[32,1792]{1,0:T(8,128)(2,1)}), bf16[512,1792]{1,0:T(8,128)(2,1)}) %all-gather.3.cloned.1.call-update) | async-done | bytes 1835024 | tf_op jit(solution)/shard_map/all_gather | solution.py:37
  82.4 8.7 %fusion.9 = f32[512,1792]{1,0:T(8,128)} fusion(bf16[512,1792]{1,0:T(8,128)(2,1)} %all-gather.3.cloned.1.call-done, bf16[1792,1792]{1,0:T(8,128)(2,1)} %param.5), kind=kOutput, calls=%fused_computation.13 | convolution fusion | flops 3288334336 | bytes 11927552 | tf_op jit(solution)/shard_map/dot_general | solution.py:38
  91.1 0.0 all-reduce.3.cloned.1.call-update
  91.1 0.0 reduce-scatter.7.cloned.1.call-start
  91.2 143.6 %all-reduce.3.cloned.1.call-done = (f32[512,1792]{1,0:T(8,128)}, f32[512,1792]{1,0:T(8,128)}) async-done(((f32[512,1792]{1,0:T(8,128)}, f32[512,1792]{1,0:T(8,128)}), (f32[512,1792]{1,0:T(8,128)}, f32[512,1792]{1,0:T(8,128)})) %all-reduce.3.cloned.1.call-update) | async-done | bytes 7340048 | tf_op jit(solution)/shard_map/psum | solution.py:38
  234.8 4.4 fusion.6
  239.2 8.1 %fusion.11 = f32[512,1792]{1,0:T(8,128)} fusion(bf16[512,1792]{1,0:T(8,128)(2,1)S(1)} %fusion.6, bf16[1792,1792]{1,0:T(8,128)(2,1)} %param.5), kind=kOutput, calls=%fused_computation.15 | convolution fusion | flops 3288334336 | bytes 11927552 | tf_op jit(solution)/shard_map/dot_general | solution.py:31
  247.3 0.0 reduce-scatter.7.cloned.1.call-update
  247.3 0.0 reduce-scatter.5.cloned.1.call-start
  247.4 9.9 %fusion.8 = f32[512,1792]{1,0:T(8,128)} fusion(bf16[1792,1792]{1,0:T(8,128)(2,1)} %param.6, f32[512,1792]{1,0:T(8,128)} %get-tuple-element.8), kind=kOutput, calls=%fused_computation.12 | convolution fusion | flops 3296591872 | bytes 13762560 | tf_op jit(solution)/shard_map/dot_general | solution.py:42
  257.3 0.0 reduce-scatter.5.cloned.1.call-update
  257.3 0.2 reduce-scatter.9.cloned.1.call-start
  257.6 8.1 %convolution_bitcast_fusion = f32[1792,1792]{0,1:T(8,128)} fusion(bf16[512,1792]{1,0:T(8,128)(2,1)S(1)} %fusion.6, bf16[512,1792]{1,0:T(8,128)(2,1)} %all-gather.3.cloned.1.call-done), kind=kOutput, calls=%fused_computation | convolution fusion | flops 3288334336 | bytes 16515072 | tf_op jit(solution)/shard_map/dot_general | solution.py:25
  265.6 0.0 copy-start
  265.6 0.0 reduce-scatter.9.cloned.1.call-update
  265.7 0.0 reduce-scatter.11.cloned.1.call-start
  265.7 1.4 copy-done
  267.2 9.7 %fusion.7 = f32[1792,1792]{1,0:T(8,128)} fusion(bf16[512,1792]{1,0:T(8,128)(2,1)S(1)} %copy-done, f32[512,1792]{1,0:T(8,128)} %get-tuple-element.8), kind=kOutput, calls=%fused_computation.11 | convolution fusion | flops 3296591872 | bytes 18350080 | tf_op jit(solution)/shard_map/dot_general | solution.py:25
  276.9 0.0 reduce-scatter.11.cloned.1.call-update
  276.9 36.7 %reduce-scatter.7.cloned.1.call-done = f32[32,1792]{1,0:T(8,128)} async-done(((f32[512,1792]{1,0:T(8,128)}), f32[32,1792]{1,0:T(8,128)}) %reduce-scatter.7.cloned.1.call-update) | async-done | bytes 229392 | tf_op jit(solution)/shard_map/reduce_scatter | solution.py:50
  313.6 1.6 convert_element_type.15
  315.2 68.3 %reduce-scatter.5.cloned.1.call-done = f32[32,1792]{1,0:T(8,128)} async-done(((f32[512,1792]{1,0:T(8,128)}), f32[32,1792]{1,0:T(8,128)}) %reduce-scatter.5.cloned.1.call-update) | async-done | bytes 229392 | tf_op jit(solution)/shard_map/reduce_scatter | solution.py:41
  383.5 1.6 convert_element_type.13
  385.1 153.0 %reduce-scatter.9.cloned.1.call-done = f32[896,1792]{0,1:T(8,128)} async-done(((f32[1792,1792]{0,1:T(8,128)}), f32[896,1792]{0,1:T(8,128)}) %reduce-scatter.9.cloned.1.call-update) | async-done | bytes 6422544 | tf_op jit(solution)/shard_map/reduce_scatter | solution.py:53
  538.1 7.8 %copy.8 = f32[896,1792]{1,0:T(8,128)} copy(f32[896,1792]{0,1:T(8,128)} %reduce-scatter.9.cloned.1.call-done) | data formatting | bytes 12845056
  545.8 146.0 %reduce-scatter.11.cloned.1.call-done = f32[896,1792]{1,0:T(8,128)} async-done(((f32[1792,1792]{1,0:T(8,128)}), f32[896,1792]{1,0:T(8,128)}) %reduce-scatter.11.cloned.1.call-update) | async-done | bytes 6422544 | tf_op jit(solution)/shard_map/reduce_scatter | solution.py:56
Async XLA Ops:
  7.2 39.9 %all-gather.5.cloned.1.call-start = ((), (), s32[]{:S(2)}) async-start(), calls=%async_computation.6 | async-start | bytes 1949696 | tf_op jit(solution)/shard_map/all_gather | solution.py:47
  7.9 74.5 %all-gather.3.cloned.1.call-start = ((), (), s32[]{:S(2)}) async-start(), calls=%async_computation.4 | async-start | bytes 1949696 | tf_op jit(solution)/shard_map/all_gather | solution.py:37
  8.6 226.2 %all-reduce.3.cloned.1.call-start = ((), (), s32[]{:S(2)}) async-start(), calls=%async_computation.10 | async-start | bytes 14680064 | tf_op jit(solution)/shard_map/psum | solution.py:38
  91.1 222.5 %reduce-scatter.7.cloned.1.call-start = ((), (), s32[]{:S(2)}) async-start(), calls=%async_computation.7 | async-start | bytes 3899392 | tf_op jit(solution)/shard_map/reduce_scatter | solution.py:50
  247.3 136.1 %reduce-scatter.5.cloned.1.call-start = ((), (), s32[]{:S(2)}) async-start(), calls=%async_computation.5 | async-start | bytes 3899392 | tf_op jit(solution)/shard_map/reduce_scatter | solution.py:41
  257.3 280.7 %reduce-scatter.9.cloned.1.call-start = ((), (), s32[]{:S(2)}) async-start(), calls=%async_computation.8 | async-start | bytes 19267584 | tf_op jit(solution)/shard_map/reduce_scatter | solution.py:53
  265.6 1.5 copy-start
  265.7 426.2 %reduce-scatter.11.cloned.1.call-start = ((), (), s32[]{:S(2)}) async-start(), calls=%async_computation.9 | async-start | bytes 19267584 | tf_op jit(solution)/shard_map/reduce_scatter | solution.py:56
Sparse Core Ops, SparseCore 0:
  9.7 37.2 all-gather.4
  48.7 33.5 all-gather.2
  91.2 143.5 all-reduce.2
  247.5 66.0 reduce-scatter.6
  316.4 67.0 reduce-scatter.4
  385.7 152.2 reduce-scatter.8
  541.1 150.7 reduce-scatter.10
where the time goes:
time: 699 us
  waiting for transfers between devices  614 us (88%)
  matrix products  53.2 us (8%)
  between operations  14.1 us (2%)
  local copies, waits for them, and re-layouts  9.21 us (1%)
  other arithmetic  7.59 us (1%)
    reduce_scatter x1, waiting for transfers between devices, local(): lax.psum_scatter(contract_lead(group, delta), 'depth', scatter_dimension=...  153 us
    reduce_scatter x1, waiting for transfers between devices, local(): lax.psum_scatter(contract_lead(activ, back), 'depth', scatter_dimension=0...  146 us
    psum x1, waiting for transfers between devices, local(): lax.psum(jnp.dot(group, first_weight, preferred_element_type=jnp.float32)...  144 us
    reduce_scatter x1, waiting for transfers between devices, local(): lax.psum_scatter(jnp.dot(activ, second_weight, preferred_element_type=jnp...  68.3 us
    all_gather x1, waiting for transfers between devices, local(): back = lax.all_gather(upstream, 'col', axis=0, tiled=True)  38.3 us
    reduce_scatter x1, waiting for transfers between devices, local(): lax.psum_scatter(contract_last(delta, first_weight), 'col', scatter_dimen...  36.7 us
    all_gather x1, waiting for transfers between devices, local(): group = lax.all_gather(tokens, 'col', axis=0, tiled=True)  26.6 us
    dot_general x2, matrix products, contract_lead(): lax.dot_general(left, right, (((0,), (0,)), ((), ())), preferred_element_...  17.8 us
  transfers between devices with their start and end apart: 7, of which 7 were waited for; matrix products, arithmetic and copies ran while one was open for 7% of the time, Pallas kernels for 0%

commit v1 on v0

v1 whole, which is shorter than its diff:
```python
import functools
import math

import jax
import jax.numpy as jnp
from jax import lax
from jax.experimental import pallas as pl
from jax.experimental.pallas import tpu as pltpu
from jax.sharding import PartitionSpec as P

MESH = pl.DeviceIdType.MESH
BF = jnp.bfloat16
F32 = jnp.float32
SCALE = math.sqrt(2.0 / math.pi)

W = 1792
H = 896
C = 256
Q = 64
B = 32
UNITS = ((0, 0), (0, 1), (1, 1), (0, 2), (1, 2), (0, 3), (1, 3), (1, 0))
OFFSET = (0, 1, 3, 2)


def gelu_and_slope(h):
    inner = SCALE * (h + 0.044715 * h * h * h)
    t = jnp.tanh(inner)
    value = 0.5 * h * (1.0 + t)
    slope = 0.5 * (1.0 + t) + 0.5 * h * (1.0 - t * t) * SCALE * (
        1.0 + 3.0 * 0.044715 * h * h
    )
    return value, slope


def kernel(
    tok_ref, w1_ref, w2_ref, up_ref,
    lo_ref, tg_ref, fg_ref, sg_ref,
    xs, wa, wb, hp, rs1s, rs1r, rs2s, rs2r, agb, slope, pdelta,
    keep, sibs, sibr, zs, zr, s0, ys, yr, facc,
    lsem, gsend, grecv, usend, urecv, fsend, frecv,
):
    x = lax.axis_index("row")
    col = lax.axis_index("col")
    yh = lax.axis_index("depth")
    z, yl, c = col // 4, (col // 2) % 2, col % 2
    y = yh * 2 + yl

    def dev(dx=0, dy=0, dz=0, dc=0):
        xx, yy = lax.rem(x + dx, 4), lax.rem(y + dy, 4)
        zz, cc = lax.rem(z + dz, 4), lax.rem(c + dc, 2)
        return (xx, zz * 4 + lax.rem(yy, 2) * 2 + cc, yy // 2)

    pending, waited = [], []

    def send(src, dst, ss, rs, to):
        cp = pltpu.make_async_remote_copy(
            src_ref=src, dst_ref=dst, send_sem=ss, recv_sem=rs,
            device_id=to, device_id_type=MESH,
        )
        cp.start()
        pending.append(cp)
        return cp

    def rows(start, size):
        return pl.ds(pl.multiple_of(start, size), size)

    half = rows(yh * H, H)
    in_copies = [
        pltpu.make_async_copy(tok_ref, xs.at[0, z, rows(c * 128 + y * B, B)], lsem.at[0]),
        pltpu.make_async_copy(up_ref, xs.at[1, z, rows(c * 128 + y * B, B)], lsem.at[1]),
        pltpu.make_async_copy(w1_ref.at[:, half], wa.at[0], lsem.at[2]),
        pltpu.make_async_copy(w2_ref.at[half, :], wb.at[0], lsem.at[3]),
    ]
    for cp in in_copies:
        cp.start()

    barrier = pltpu.get_barrier_semaphore()
    peers = [dev(dc=1), dev(dx=1), dev(dx=3), dev(dy=1), dev(dy=2), dev(dy=3),
             dev(dz=1), dev(dz=2), dev(dz=3)]
    for p in peers:
        pl.semaphore_signal(barrier, inc=1, device_id=p, device_id_type=MESH)
    pl.semaphore_wait(barrier, len(peers))

    G = {}

    def gsem(k, i):
        return gsend.at[k, i], grecv.at[k, i]

    def gather_y(k):
        in_copies[k].wait()
        blk = xs.at[k, z, rows(c * 128 + y * B, B)]
        for d in (1, 3, 2):
            G[k, "y", d] = send(blk, blk, *gsem(k, d - 1), dev(dy=d))

    def gather_z(k):
        for d in (1, 3, 2):
            G[k, "y", d].wait_recv()
        grp = xs.at[k, z, rows(c * 128, 128)]
        G[k, "s", 0] = send(grp, grp, *gsem(k, 3), dev(dc=1))
        G[k, "z", 1] = send(grp, grp, *gsem(k, 4), dev(dz=1))
        G[k, "z", 3] = send(grp, grp, *gsem(k, 5), dev(dz=3))

    def gather_relay(k, chunk):
        zz = lax.rem(z + OFFSET[chunk], 4)
        G[k, "z", 3 if chunk == 1 else 1].wait_recv()
        if chunk == 1:
            part = xs.at[k, zz, rows(c * 128 + 64, 64)]
            G[k, "r", 1] = send(part, part, *gsem(k, 6), dev(dz=3))
        else:
            part = xs.at[k, zz, rows(c * 128, 64)]
            G[k, "r", 2] = send(part, part, *gsem(k, 7), dev(dz=1))
        grp = xs.at[k, zz, rows(c * 128, 128)]
        G[k, "s", chunk] = send(grp, grp, *gsem(k, 7 + chunk), dev(dc=1))

    def gather_last(k):
        G[k, "r", 1].wait_recv()
        G[k, "r", 2].wait_recv()
        grp = xs.at[k, lax.rem(z + 2, 4), rows(c * 128, 128)]
        G[k, "s", 3] = send(grp, grp, *gsem(k, 10), dev(dc=1))

    def gather_done(k, chunk):
        G[k, "s", chunk].wait_recv()

    U = {}

    def usem(u, i):
        return usend.at[u, i], urecv.at[u, i]

    def stage_a(u):
        kind, chunk = UNITS[u]
        zz = lax.rem(z + OFFSET[chunk], 4)
        slot = u % 3

        def tile(n, width):
            at = pl.ds(n, width)
            hp[slot, :, at] = jnp.dot(
                xs[kind, zz], wa[kind, :, at], preferred_element_type=F32
            )

        @pl.loop(0, 3)
        def _(i):
            tile(pl.multiple_of(i * 256, 256), 256)

        tile(768, 128)
        rs1s[u] = hp[slot, rows(lax.rem(x + 2, 4) * Q, Q)].astype(BF)
        U[u, "a", 0] = send(rs1s.at[u, 0:32], rs1r.at[u, 0], *usem(u, 0), dev(dx=1))
        U[u, "a", 1] = send(rs1s.at[u, 32:64], rs1r.at[u, 1], *usem(u, 1), dev(dx=3))

    def stage_b(u):
        slot = u % 3
        to_right = lax.rem(x + 1, 4) * Q
        to_left = lax.rem(x + 3, 4) * Q
        U[u, "a", 0].wait_recv()
        rs2s[u, 0, 0:32] = (hp[slot, rows(to_right, 32)] + rs1r[u, 0].astype(F32)).astype(BF)
        rs2s[u, 0, 32:64] = hp[slot, rows(to_right + 32, 32)].astype(BF)
        U[u, "b", 0] = send(rs2s.at[u, 0], rs2r.at[u, 0], *usem(u, 2), dev(dx=1))
        U[u, "a", 1].wait_recv()
        rs2s[u, 1, 0:32] = hp[slot, rows(to_left, 32)].astype(BF)
        rs2s[u, 1, 32:64] = (hp[slot, rows(to_left + 32, 32)] + rs1r[u, 1].astype(F32)).astype(BF)
        U[u, "b", 1] = send(rs2s.at[u, 1], rs2r.at[u, 1], *usem(u, 3), dev(dx=3))

    def stage_c(u):
        kind, chunk = UNITS[u]
        slot = u % 3
        U[u, "b", 0].wait_recv()
        U[u, "b", 1].wait_recv()
        for r in range(0, Q, 32):
            h = hp[slot, rows(x * Q + r, 32)]
            h = h + rs2r[u, 0, r : r + 32].astype(F32) + rs2r[u, 1, r : r + 32].astype(F32)
            if kind == 0:
                value, sl = gelu_and_slope(h)
                slope[chunk, r : r + 32] = sl
            else:
                value = h * slope[chunk, r : r + 32]
            agb[u, rows(x * Q + r, 32)] = value.astype(BF)
        mine = agb.at[u, rows(x * Q, Q)]
        U[u, "c", 0] = send(mine, mine, *usem(u, 4), dev(dx=1))
        U[u, "c", 1] = send(mine, mine, *usem(u, 5), dev(dx=3))

    def stage_d(u):
        U[u, "c", 0].wait_recv()
        part = agb.at[u, rows(lax.rem(x + 3, 4) * Q, 32)]
        U[u, "d", 0] = send(part, part, *usem(u, 6), dev(dx=1))
        U[u, "c", 1].wait_recv()
        part = agb.at[u, rows(lax.rem(x + 1, 4) * Q + 32, 32)]
        U[u, "d", 1] = send(part, part, *usem(u, 7), dev(dx=3))

    def stage_e(u):
        kind, chunk = UNITS[u]
        U[u, "d", 0].wait_recv()
        U[u, "d", 1].wait_recv()
        if kind == 1:
            U[u, "p"] = send(agb.at[u], pdelta.at[chunk], *usem(u, 8), dev(dy=2))
        away, own = rows((1 - c) * 128, 128), rows(c * 128, 128)
        if u >= 4:
            U[u - 4, "e"].wait_send()
            waited.append(id(U[u - 4, "e"]))

        @pl.loop(0, W // 256)
        def _(i):
            at = pl.ds(pl.multiple_of(i * 256, 256), 256)
            lhs = jnp.concatenate([agb[u, away], agb[u, own]], axis=0)
            part = jnp.dot(lhs, wb[kind, :, at], preferred_element_type=F32)
            sibs[u % 4, :, at] = part[:128].astype(BF)
            keep[u % 2, :, at] = part[128:]

        U[u, "e"] = send(sibs.at[u % 4], sibr.at[u], *usem(u, 9), dev(dc=1))

    def stage_f(u):
        kind, chunk = UNITS[u]
        U[u, "e"].wait_recv()

        @pl.loop(0, 4)
        def _(i):
            r = rows(i * 32, 32)
            total = keep[u % 2, r] + sibr[u, r].astype(F32)
            if chunk == 0:
                s0[kind, r] = total
            else:
                zs[kind, chunk - 1, r] = total.astype(BF)

        if chunk != 0:
            U[kind, chunk, "z"] = send(
                zs.at[kind, chunk - 1], zr.at[kind, chunk - 1], *usem(u, 10),
                dev(dz=OFFSET[chunk]),
            )

    def stage_g(kind):
        for chunk in (1, 2, 3):
            U[kind, chunk, "z"].wait_recv()

        def total(blk):
            r = rows(blk * B, B)
            t = s0[kind, r]
            for i in range(3):
                t = t + zr[kind, i, r].astype(F32)
            return t

        for d in (1, 3, 2):
            ys[kind, d] = total(lax.rem(y + d, 4)).astype(BF)
            U[kind, d, "y"] = send(
                ys.at[kind, d], yr.at[kind, d - 1], fsend.at[kind, d - 1],
                frecv.at[kind, d - 1], dev(dy=d),
            )
        s0[kind, 0:B] = total(y)

    def stage_h(kind):
        t = s0[kind, 0:B]
        for d in (1, 3, 2):
            U[kind, d, "y"].wait_recv()
            t = t + yr[kind, d - 1].astype(F32)
        (lo_ref, tg_ref)[kind][...] = t.astype(BF)

    def lead(a, b):
        return lax.dot_general(a, b, (((0,), (0,)), ((), ())), preferred_element_type=F32)

    acts = [UNITS.index((0, j)) for j in range(4)]

    def second_grad():
        @pl.loop(0, W // 256)
        def _(i):
            at = pl.ds(pl.multiple_of(i * 256, 256), 256)
            t = None
            for j in range(4):
                p = lead(agb[acts[j]], xs[1, lax.rem(z + OFFSET[j], 4), :, at])
                t = p if t is None else t + p
            wb[0, :, at] = t.astype(BF)

        cp = pltpu.make_async_copy(wb.at[0], sg_ref, lsem.at[4])
        cp.start()
        return cp

    def first_grad(chunk, own, first, last):
        src = agb.at[UNITS.index((1, chunk))] if own else pdelta.at[chunk]
        side = 0 if own else 1
        zz = lax.rem(z + OFFSET[chunk], 4)

        def tile(n, width):
            at = pl.ds(n, width)
            p = lead(xs[0, zz, :, half], src[:, at])
            if not first:
                p = p + facc[side, :, at]
            if last:
                wa[0, side * H : side * H + H, at] = p.astype(BF)
            else:
                facc[side, :, at] = p

        @pl.loop(0, 3)
        def _(i):
            tile(pl.multiple_of(i * 256, 256), 256)

        tile(768, 128)
        if last:
            to = rows((yh if own else 1 - yh) * H, H)
            cp = pltpu.make_async_copy(
                wa.at[0, side * H : side * H + H], fg_ref.at[:, to], lsem.at[5 + side]
            )
            cp.start()
            return cp

    gather_y(0)
    gather_y(1)
    in_copies[3].wait()

    @pl.loop(0, W // 256)
    def _(i):
        at = pl.ds(pl.multiple_of(i * 256, 256), 256)
        wa[1, at, :] = wb[0, :, at].T

    gather_z(0)
    gather_z(1)
    in_copies[2].wait()

    @pl.loop(0, W // 256)
    def _(i):
        at = pl.ds(pl.multiple_of(i * 256, 256), 256)
        wb[1, :, at] = wa[0, at, :].T

    gather_done(0, 0)
    stage_a(0)
    stage_b(0)
    stage_c(0)
    stage_d(0)
    gather_done(1, 0)
    gather_relay(0, 1)
    gather_relay(0, 2)
    gather_done(0, 1)
    stage_a(1)
    stage_e(0)
    stage_b(1)
    gather_relay(1, 1)
    gather_relay(1, 2)
    gather_done(1, 1)
    stage_a(2)
    stage_f(0)
    stage_c(1)
    stage_b(2)
    gather_last(0)
    gather_done(0, 2)
    stage_a(3)
    stage_d(1)
    stage_c(2)
    stage_b(3)
    stage_e(1)
    gather_last(1)
    gather_done(1, 2)
    stage_a(4)
    stage_d(2)
    stage_c(3)
    stage_b(4)
    stage_f(1)
    stage_e(2)
    gather_done(0, 3)
    stage_a(5)
    stage_d(3)
    stage_c(4)
    stage_b(5)
    stage_f(2)
    stage_e(3)
    gather_done(1, 3)
    stage_a(6)
    stage_d(4)
    stage_c(5)
    stage_b(6)
    stage_f(3)
    stage_e(4)
    first_grad(1, True, True, False)
    stage_a(7)
    stage_d(5)
    stage_c(6)
    stage_b(7)
    stage_f(4)
    stage_e(5)
    first_grad(2, True, False, False)
    U[2, "p"].wait_recv()
    first_grad(1, False, True, False)
    stage_d(6)
    stage_c(7)
    stage_f(5)
    stage_e(6)
    out = [second_grad()]
    stage_d(7)
    stage_f(6)
    stage_e(7)
    first_grad(3, True, False, False)
    stage_g(0)
    stage_f(7)
    stage_g(1)
    U[4, "p"].wait_recv()
    first_grad(2, False, False, False)
    out.append(first_grad(0, True, False, True))
    stage_h(0)
    U[6, "p"].wait_recv()
    first_grad(3, False, False, False)
    stage_h(1)
    U[7, "p"].wait_recv()
    out.append(first_grad(0, False, False, True))
    for cp in pending:
        if id(cp) not in waited:
            cp.wait_send()
    for cp in out:
        cp.wait()


def local(tokens, first_weight, second_weight, upstream):
    vm = pl.BlockSpec(memory_space=pltpu.VMEM)
    hbm = pl.BlockSpec(memory_space=pl.ANY)
    dma = pltpu.SemaphoreType.DMA
    lo, tg, fg, sg = pl.pallas_call(
        kernel,
        out_shape=(
            jax.ShapeDtypeStruct((B, W), BF),
            jax.ShapeDtypeStruct((B, W), BF),
            jax.ShapeDtypeStruct((H, W), BF),
            jax.ShapeDtypeStruct((H, W), BF),
        ),
        in_specs=[hbm] * 4,
        out_specs=(vm, vm, hbm, hbm),
        scratch_shapes=[
            pltpu.VMEM((2, 4, C, W), BF),
            pltpu.VMEM((2, W, H), BF),
            pltpu.VMEM((2, H, W), BF),
            pltpu.VMEM((3, C, H), F32),
            pltpu.VMEM((8, Q, H), BF),
            pltpu.VMEM((8, 2, 32, H), BF),
            pltpu.VMEM((8, 2, Q, H), BF),
            pltpu.VMEM((8, 2, Q, H), BF),
            pltpu.VMEM((8, C, H), BF),
            pltpu.VMEM((4, Q, H), F32),
            pltpu.VMEM((4, C, H), BF),
            pltpu.VMEM((2, 128, W), F32),
            pltpu.VMEM((4, 128, W), BF),
            pltpu.VMEM((8, 128, W), BF),
            pltpu.VMEM((2, 3, 128, W), BF),
            pltpu.VMEM((2, 3, 128, W), BF),
            pltpu.VMEM((2, 128, W), F32),
            pltpu.VMEM((2, 4, B, W), BF),
            pltpu.VMEM((2, 3, B, W), BF),
            pltpu.VMEM((2, H, H), F32),
            dma((7,)),
            dma((2, 11)), dma((2, 11)),
            dma((8, 11)), dma((8, 11)),
            dma((2, 3)), dma((2, 3)),
        ],
        compiler_params=pltpu.CompilerParams(
            collective_id=0, has_side_effects=True, vmem_limit_bytes=60 << 20
        ),
        cost_estimate=pl.CostEstimate(
            flops=6 * 2 * 1024 * W * H, bytes_accessed=16 << 20, transcendentals=0
        ),
        name="ffn",
    )(tokens, first_weight, second_weight, upstream)
    return lo, tg, fg.astype(F32), sg.astype(F32)


def solution(mesh):
    in_specs = (
        P(("col", "depth"), "row"),
        P("row", "col"),
        P("col", "row"),
        P(("col", "depth"), "row"),
    )
    out_specs = (
        P(("col", "depth"), "row"),
        P(("col", "depth"), "row"),
        P(("row", "depth"), "col"),
        P(("col", "depth"), "row"),
    )
    return jax.shard_map(local, mesh=mesh, in_specs=in_specs, out_specs=out_specs, check_vma=False)
```

time: 699 us -> 144 us (0.21)
  waiting for transfers between devices: 614 us -> 0 us
  Pallas kernels: 0 us -> 132 us
  matrix products: 53.2 us -> 0 us
  between operations: 14.1 us -> 0.65 us
  local copies, waits for them, and re-layouts: 9.21 us -> 1.3 us
    reduce_scatter x4 -> x0, waiting for transfers between devices: 404 us -> none  [the longest x1 153 us: local(): lax.psum_scatter(contract_lead(group, delta), 'depth', scatter_dimension=...]
    psum x1 -> x0, waiting for transfers between devices: 144 us -> none  [local(): lax.psum(jnp.dot(group, first_weight, preferred_element_type=jnp.float32)...]
    pallas_call x0 -> x1, Pallas kernels: none -> 132 us  [local(): pl.pallas_call(kernel, out_shape=(jax.ShapeDtypeStruct((B, W), BF), jax.S...]
    all_gather x2 -> x0, waiting for transfers between devices: 64.9 us -> none  [the longest x1 38.3 us: local(): back = lax.all_gather(upstream, 'col', axis=0, tiled=True)]
    dot_general x6 -> x0, matrix products: 53.2 us -> none  [the longest x2 17.8 us: contract_lead(): lax.dot_general(left, right, (((0,), (0,)), ((), ())), preferred_element_...]
    unnamed x3 -> x8, local copies, waits for them, and re-layouts: 9.21 us -> 1.3 us
  transfers between devices with their start and end apart: 7 -> 0, of which waited for: 7 -> 0; matrix products, arithmetic and copies ran while one was open for 7% -> 0% of each run, Pallas kernels for 0% -> 0%
where the time goes in v1:
time: 144 us; the launch traced here: 142 us
  Pallas kernels  132 us (92%)
  other arithmetic  8.5 us (6%)
    pallas_call x1, Pallas kernels, local(): pl.pallas_call(kernel, out_shape=(jax.ShapeDtypeStruct((B, W), BF), jax.S...  132 us
    convert_element_type x2, other arithmetic, local(): return (lo, tg, fg.astype(F32), sg.astype(F32))  8.5 us

profile of v1, /device:TPU:1, one launch (start us, length us, event | category | flops | bytes accessed | tf_op | source)
XLA Modules:
  0.0 142.2 jit_solution(16976804725531180160)
XLA Ops:
  0.6 131.7 %ffn.1 = (bf16[32,1792]{1,0:T(8,128)(2,1)}, bf16[32,1792]{1,0:T(8,128)(2,1)}, bf16[896,1792]{1,0:T(8,128)(2,1)}, bf16[896,1792]{1,0:T(8,128)(2,1)}) custom-call(bf16[32,1792]{1,0:T(8,128)(2,1)} %tok_ref.1, bf16[1792,1792]{1,0:T(8,128)(2,1)} %w1_ref.1, bf16[1792,1792]{1,0:T(8,128)(2,1)} %w2_ref.1, bf16[32,1792]{1,0:T(8,128)(2,1)} %up_ref.1), custom_call_target="tpu_custom_call" | custom-call | flops 19730006016 | bytes 16777216 | tf_op jit(solution)/shard_map/ffn/pallas_call | solution.py:409
  132.3 0.0 copy-start
  132.4 5.3 %convert_element_type.6 = f32[896,1792]{1,0:T(8,128)} convert(bf16[896,1792]{1,0:T(8,128)(2,1)} %get-tuple-element.10) | non-fusion elementwise | flops 1605632 | bytes 9633792 | tf_op jit(solution)/shard_map/convert_element_type | solution.py:453
  137.6 0.0 copy-done
  137.6 0.0 copy-start.2
  137.6 0.0 copy-start.1
  137.6 3.2 %convert_element_type.7 = f32[896,1792]{1,0:T(8,128)} convert(bf16[896,1792]{1,0:T(8,128)(2,1)S(1)} %copy-done) | non-fusion elementwise | flops 1605632 | bytes 9633792 | tf_op jit(solution)/shard_map/convert_element_type | solution.py:453
  140.9 0.0 copy-done.2
  140.9 0.6 copy.10
  141.5 0.0 copy-done.1
  141.5 0.6 copy.11
Async XLA Ops:
  132.3 5.3 %copy-start = (bf16[896,1792]{1,0:T(8,128)(2,1)S(1)}, bf16[896,1792]{1,0:T(8,128)(2,1)}, u32[]{:S(2)}) copy-start(bf16[896,1792]{1,0:T(8,128)(2,1)} %get-tuple-element.11) | copy-start | bytes 9633796
  137.6 3.2 %copy-start.2 = (bf16[32,1792]{1,0:T(8,128)(2,1)S(1)}, bf16[32,1792]{1,0:T(8,128)(2,1)}, u32[]{:S(2)}) copy-start(bf16[32,1792]{1,0:T(8,128)(2,1)} %get-tuple-element.16) | copy-start | bytes 344068
  137.6 3.9 %copy-start.1 = (bf16[32,1792]{1,0:T(8,128)(2,1)S(1)}, bf16[32,1792]{1,0:T(8,128)(2,1)}, u32[]{:S(2)}) copy-start(bf16[32,1792]{1,0:T(8,128)(2,1)} %get-tuple-element.17) | copy-start | bytes 344068

commit v2 on v1

v2 whole, which is shorter than its diff:
```python
import math

import jax
import jax.numpy as jnp
from jax import lax
from jax.experimental import pallas as pl
from jax.experimental.pallas import tpu as pltpu
from jax.sharding import PartitionSpec as P

MESH = pl.DeviceIdType.MESH
BF = jnp.bfloat16
F32 = jnp.float32
SCALE = math.sqrt(2.0 / math.pi)

W = 1792
H = 896
C = 256
Q = 64
B = 32
OFFSET = (0, 1, 3, 2)
DIRECT_SUM = ((0, 0), (1, 0))
DIRECT_GATHER = ((1, 0), (1, 1))
DIRECT_Z = ()
FS, KS, SS = 3, 4, 4
RELAY_Z = (0, 1)
F1 = (0, 1, 2)

SCHEDULE = (
    ("gy", 0), ("gy", 1), ("gz", 0), ("a", 0, 0), ("gr", 0, 2), ("gr", 0, 1), ("c", 0, 0),
    ("gz", 1), ("a", 0, 2), ("a", 0, 1), ("d", 0, 0), ("gl", 0), ("b", 0, 2), ("a", 0, 3),
    ("b", 0, 1), ("b", 0, 3), ("t1",), ("c", 0, 2), ("t2",), ("gr", 1, 1), ("gr", 1, 2),
    ("c", 0, 3), ("c", 0, 1), ("a", 1, 1), ("d", 0, 3), ("gl", 1), ("a", 1, 2), ("a", 1, 3),
    ("d", 0, 2), ("e", 0, 3), ("d", 0, 1), ("b", 1, 3), ("b", 1, 2), ("f", 0, 3), ("e", 0, 2),
    ("e", 0, 1), ("c", 1, 3), ("b", 1, 1), ("e", 0, 0), ("f", 0, 1), ("f", 0, 2), ("d", 1, 3),
    ("c", 1, 2), ("c", 1, 1), ("p", 1, 3), ("e", 1, 3), ("d", 1, 2), ("a", 1, 0), ("f", 1, 3),
    ("f", 0, 0), ("sg", 0), ("e", 1, 1), ("e", 1, 2), ("f1s", 1, 2), ("f", 1, 1), ("f", 1, 2),
    ("c", 1, 0), ("fo", 3), ("sg", 1), ("f1r", 1, 2), ("f1s", 1, 0), ("g", 0), ("f1s", 1, 1),
    ("e", 1, 0), ("fo", 1), ("f", 1, 0), ("g", 1), ("fp", 2), ("fo", 2), ("fp", 0), ("fo", 0),
    ("fp", 3), ("fp", 1), ("h", 0), ("h", 1),
)


def gelu_and_slope(h):
    inner = SCALE * (h + 0.044715 * h * h * h)
    t = jnp.tanh(inner)
    value = 0.5 * h * (1.0 + t)
    slope = 0.5 * (1.0 + t) + 0.5 * h * (1.0 - t * t) * SCALE * (
        1.0 + 3.0 * 0.044715 * h * h
    )
    return value, slope


def kernel(
    tok_ref, w1_ref, w2_ref, up_ref,
    lo_ref, tg_ref, fg_ref, sg_ref,
    xs, wa, wb, hp, rs1s, rs1r, rs2s, rs2r, agb, slope, pdelta,
    keep, sibs, sibr, zs, zr, s0, ys, yr, facc,
    lsem, gsend, grecv, usend, urecv, fsend, frecv,
):
    x = lax.axis_index("row")
    col = lax.axis_index("col")
    yh = lax.axis_index("depth")
    z, yl, c = col // 4, (col // 2) % 2, col % 2
    y = yh * 2 + yl

    def dev(dx=0, dy=0, dz=0, dc=0):
        xx, yy = lax.rem(x + dx, 4), lax.rem(y + dy, 4)
        zz, cc = lax.rem(z + dz, 4), lax.rem(c + dc, 2)
        return (xx, zz * 4 + lax.rem(yy, 2) * 2 + cc, yy // 2)

    pending, waited = [], []

    def send(src, dst, ss, rs, to):
        cp = pltpu.make_async_remote_copy(
            src_ref=src, dst_ref=dst, send_sem=ss, recv_sem=rs,
            device_id=to, device_id_type=MESH,
        )
        cp.start()
        pending.append(cp)
        return cp

    def rows(start, size):
        return pl.ds(pl.multiple_of(start, size), size)

    half = rows(yh * H, H)
    in_copies = [
        pltpu.make_async_copy(tok_ref, xs.at[0, z, rows(c * 128 + y * B, B)], lsem.at[0]),
        pltpu.make_async_copy(up_ref, xs.at[1, z, rows(c * 128 + y * B, B)], lsem.at[1]),
        pltpu.make_async_copy(w1_ref.at[:, half], wa.at[0], lsem.at[2]),
        pltpu.make_async_copy(w2_ref.at[half, :], wb.at[0], lsem.at[3]),
    ]
    for cp in in_copies:
        cp.start()
    loaded = set()

    def ready(i):
        if i not in loaded:
            loaded.add(i)
            in_copies[i].wait()

    barrier = pltpu.get_barrier_semaphore()
    peers = [dev(dc=1), dev(dx=1), dev(dx=2), dev(dx=3), dev(dy=1), dev(dy=2), dev(dy=3),
             dev(dz=1), dev(dz=2), dev(dz=3)]
    for p in peers:
        pl.semaphore_signal(barrier, inc=1, device_id=p, device_id_type=MESH)
    pl.semaphore_wait(barrier, len(peers))

    G = {}

    def gsem(k, i):
        return gsend.at[k, i], grecv.at[k, i]

    def gather_y(k):
        ready(k)
        blk = xs.at[k, z, rows(c * 128 + y * B, B)]
        for d in (1, 3, 2):
            G[k, "y", d] = send(blk, blk, *gsem(k, d - 1), dev(dy=d))

    def gather_z(k):
        for d in (1, 3, 2):
            G[k, "y", d].wait_recv()
        grp = xs.at[k, z, rows(c * 128, 128)]
        G[k, "s", 0] = send(grp, grp, *gsem(k, 3), dev(dc=1))
        G[k, "z", 1] = send(grp, grp, *gsem(k, 4), dev(dz=1))
        G[k, "z", 3] = send(grp, grp, *gsem(k, 5), dev(dz=3))
        if k in DIRECT_Z:
            G[k, "r", 1] = send(grp, grp, *gsem(k, 6), dev(dz=2))

    def gather_relay(k, chunk):
        zz = lax.rem(z + OFFSET[chunk], 4)
        G[k, "z", 3 if chunk == 1 else 1].wait_recv()
        if k in DIRECT_Z:
            pass
        elif chunk == 1:
            part = xs.at[k, zz, rows(c * 128 + 64, 64)]
            G[k, "r", 1] = send(part, part, *gsem(k, 6), dev(dz=3))
        else:
            part = xs.at[k, zz, rows(c * 128, 64)]
            G[k, "r", 2] = send(part, part, *gsem(k, 7), dev(dz=1))
        grp = xs.at[k, zz, rows(c * 128, 128)]
        G[k, "s", chunk] = send(grp, grp, *gsem(k, 7 + chunk), dev(dc=1))

    def gather_last(k):
        G[k, "r", 1].wait_recv()
        if k not in DIRECT_Z:
            G[k, "r", 2].wait_recv()
        grp = xs.at[k, lax.rem(z + 2, 4), rows(c * 128, 128)]
        G[k, "s", 3] = send(grp, grp, *gsem(k, 10), dev(dc=1))

    grouped = set()

    def group(k, chunk):
        if (k, chunk) not in grouped:
            grouped.add((k, chunk))
            G[k, "s", chunk].wait_recv()

    U = {}
    free_f, free_k, sib_sends = list(range(FS)), list(range(KS)), []
    slot_f, slot_k = {}, {}

    def usem(u, i):
        n = u[0] * 4 + u[1]
        return usend.at[n, i], urecv.at[n, i]

    def buf(ref, u):
        return ref.at[u[0] * 4 + u[1]]

    def stage_a(*u):
        kind, chunk = u
        group(kind, chunk)
        if kind == 0:
            ready(2)
        zz = lax.rem(z + OFFSET[chunk], 4)
        f = hp.at[slot_f.setdefault(u, free_f.pop(0))]
        f[...] = jnp.dot(xs[kind, zz], wa[kind], preferred_element_type=F32)
        away, into = buf(rs1s, u), buf(rs1r, u)
        away[...] = f[rows(lax.rem(x + 2, 4) * Q, Q)].astype(BF)
        if u in DIRECT_SUM:
            U[u, "a", 0] = send(away, into, *usem(u, 0), dev(dx=2))
            out, into = buf(rs2s, u), buf(rs2r, u)
            out[0] = f[rows(lax.rem(x + 1, 4) * Q, Q)].astype(BF)
            U[u, "b", 0] = send(out.at[0], into.at[0], *usem(u, 2), dev(dx=1))
            out[1] = f[rows(lax.rem(x + 3, 4) * Q, Q)].astype(BF)
            U[u, "b", 1] = send(out.at[1], into.at[1], *usem(u, 3), dev(dx=3))
            return
        U[u, "a", 0] = send(away.at[0:32], into.at[0:32], *usem(u, 0), dev(dx=1))
        U[u, "a", 1] = send(away.at[32:64], into.at[32:64], *usem(u, 1), dev(dx=3))

    def stage_b(*u):
        f = hp.at[slot_f[u]]
        right, left = lax.rem(x + 1, 4) * Q, lax.rem(x + 3, 4) * Q
        out, got, into = buf(rs2s, u), buf(rs1r, u), buf(rs2r, u)
        U[u, "a", 0].wait_recv()
        out[0, 0:32] = (f[rows(right, 32)] + got[0:32].astype(F32)).astype(BF)
        out[0, 32:64] = f[rows(right + 32, 32)].astype(BF)
        U[u, "b", 0] = send(out.at[0], into.at[0], *usem(u, 2), dev(dx=1))
        U[u, "a", 1].wait_recv()
        out[1, 0:32] = f[rows(left, 32)].astype(BF)
        out[1, 32:64] = (f[rows(left + 32, 32)] + got[32:64].astype(F32)).astype(BF)
        U[u, "b", 1] = send(out.at[1], into.at[1], *usem(u, 3), dev(dx=3))

    def stage_c(*u):
        kind, chunk = u
        f, got, ag = hp.at[slot_f[u]], buf(rs2r, u), buf(agb, u)
        U[u, "b", 0].wait_recv()
        U[u, "b", 1].wait_recv()
        if u in DIRECT_SUM:
            U[u, "a", 0].wait_recv()
        for r in range(0, Q, 32):
            h = f[rows(x * Q + r, 32)]
            h = h + got[0, r : r + 32].astype(F32) + got[1, r : r + 32].astype(F32)
            if u in DIRECT_SUM:
                h = h + buf(rs1r, u)[r : r + 32].astype(F32)
            if kind == 0:
                value, sl = gelu_and_slope(h)
                slope[chunk, r : r + 32] = sl
            else:
                value = h * slope[chunk, r : r + 32]
            ag[rows(x * Q + r, 32)] = value.astype(BF)
        free_f.append(slot_f[u])
        mine = ag.at[rows(x * Q, Q)]
        if kind == 1 and chunk in F1:
            U[u, "p"] = send(mine, pdelta.at[chunk, rows(x * Q, Q)], *usem(u, 8), dev(dy=2))
        if u in DIRECT_GATHER:
            U[u, "d", 0] = send(mine, mine, *usem(u, 6), dev(dx=2))
        U[u, "c", 0] = send(mine, mine, *usem(u, 4), dev(dx=1))
        U[u, "c", 1] = send(mine, mine, *usem(u, 5), dev(dx=3))

    def stage_d(*u):
        ag = buf(agb, u)
        U[u, "c", 0].wait_recv()
        part = ag.at[rows(lax.rem(x + 3, 4) * Q, 32)]
        U[u, "d", 0] = send(part, part, *usem(u, 6), dev(dx=1))
        U[u, "c", 1].wait_recv()
        part = ag.at[rows(lax.rem(x + 1, 4) * Q + 32, 32)]
        U[u, "d", 1] = send(part, part, *usem(u, 7), dev(dx=3))

    def stage_f1s(*u):
        part = pdelta.at[u[1], rows(x * Q, Q)]
        U[u, "p"].wait_recv()
        if u in DIRECT_GATHER:
            U[u, "pd", 0] = send(part, part, *usem(u, 14), dev(dx=2))
        U[u, "pc", 0] = send(part, part, *usem(u, 12), dev(dx=1))
        U[u, "pc", 1] = send(part, part, *usem(u, 13), dev(dx=3))

    def stage_f1r(*u):
        U[u, "pc", 0].wait_recv()
        part = pdelta.at[u[1], rows(lax.rem(x + 3, 4) * Q, 32)]
        U[u, "pd", 0] = send(part, part, *usem(u, 14), dev(dx=1))
        U[u, "pc", 1].wait_recv()
        part = pdelta.at[u[1], rows(lax.rem(x + 1, 4) * Q + 32, 32)]
        U[u, "pd", 1] = send(part, part, *usem(u, 15), dev(dx=3))

    gathered = set()

    def whole(u):
        if u not in gathered:
            gathered.add(u)
            U[u, "d", 0].wait_recv()
            if u in DIRECT_GATHER:
                U[u, "c", 0].wait_recv()
                U[u, "c", 1].wait_recv()
            else:
                U[u, "d", 1].wait_recv()

    def stage_p(*u):
        whole(u)
        U[u, "p"] = send(buf(agb, u), pdelta.at[u[1]], *usem(u, 8), dev(dy=2))

    def stage_e(*u):
        kind = u[0]
        whole(u)
        if kind == 0:
            ready(3)
        n = len(sib_sends)
        if n >= SS:
            sib_sends[n - SS].wait_send()
            waited.append(id(sib_sends[n - SS]))
        out, k = sibs.at[n % SS], keep.at[slot_k.setdefault(u, free_k.pop(0))]
        ag = buf(agb, u)
        lhs = jnp.concatenate(
            [ag[rows((1 - c) * 128, 128)], ag[rows(c * 128, 128)]], axis=0
        )
        part = jnp.dot(lhs, wb[kind], preferred_element_type=F32)
        out[...] = part[:128].astype(BF)
        U[u, "e"] = send(out, buf(sibr, u), *usem(u, 9), dev(dc=1))
        k[...] = part[128:]
        sib_sends.append(U[u, "e"])

    def stage_f(*u):
        kind, chunk = u
        U[u, "e"].wait_recv()
        k, got = keep.at[slot_k[u]], buf(sibr, u)
        relayed = kind in RELAY_Z and chunk in (1, 2)
        if relayed:
            U[kind, chunk, "zr"].wait_recv()
        for n in range(4):
            r = slice(n * B, n * B + B)
            total = k[r] + got[r].astype(F32)
            if relayed and n // 2 == chunk - 1:
                total = total + zr[kind, 2, r].astype(F32)
            if chunk == 0:
                s0[kind, r] = total
            else:
                zs[kind, chunk - 1, r] = total.astype(BF)
        free_k.append(slot_k[u])
        if kind in RELAY_Z and chunk == 3:
            for i, d in ((1, 1), (2, 3)):
                r = slice(i * 64 - 64, i * 64)
                U[kind, i, "zr"] = send(
                    zs.at[kind, 2, r], zr.at[kind, 2, r], *usem((kind, i), 11), dev(dz=d)
                )
        elif chunk != 0:
            U[kind, chunk, "z"] = send(
                zs.at[kind, chunk - 1], zr.at[kind, chunk - 1], *usem(u, 10),
                dev(dz=OFFSET[chunk]),
            )

    def stage_g(kind):
        parts = (1, 2) if kind in RELAY_Z else (1, 2, 3)
        for chunk in parts:
            U[kind, chunk, "z"].wait_recv()

        def total(blk):
            r = rows(blk * B, B)
            t = s0[kind, r]
            for i in parts:
                t = t + zr[kind, i - 1, r].astype(F32)
            return t

        for d in (1, 3, 2):
            ys[kind, d - 1] = total(lax.rem(y + d, 4)).astype(BF)
            U[kind, d, "y"] = send(
                ys.at[kind, d - 1], yr.at[kind, d - 1], fsend.at[kind, d - 1],
                frecv.at[kind, d - 1], dev(dy=d),
            )
        s0[kind, 0:B] = total(y)

    def stage_h(kind):
        t = s0[kind, 0:B]
        for d in (1, 3, 2):
            U[kind, d, "y"].wait_recv()
            t = t + yr[kind, d - 1].astype(F32)
        (lo_ref, tg_ref)[kind][...] = t.astype(BF)

    out_copies = []
    count = [0, 0]

    def lead(a, b):
        return lax.dot_general(a, b, (((0,), (0,)), ((), ())), preferred_element_type=F32)

    def stage_sg(part):
        at = slice(part * H, part * H + H)
        t = None
        for j in range(4):
            whole((0, j))
            group(1, j)
            p = lead(agb[j], xs[1, lax.rem(z + OFFSET[j], 4), :, at])
            t = p if t is None else t + p
        wb[0, :, at] = t.astype(BF)
        cp = pltpu.make_async_copy(wb.at[0, :, at], sg_ref.at[:, at], lsem.at[4 + part])
        cp.start()
        out_copies.append(cp)

    def first_grad(chunk, side, src):
        p = lead(xs[0, lax.rem(z + OFFSET[chunk], 4), :, half], src[...])
        if count[side]:
            p = p + facc[side]
        count[side] += 1
        if count[side] < 4:
            facc[side] = p
            return
        at = slice(side * H, side * H + H)
        wa[0, at, :] = p.astype(BF)
        to = rows((1 - yh if side else yh) * H, H)
        cp = pltpu.make_async_copy(wa.at[0, at], fg_ref.at[:, to], lsem.at[6 + side])
        cp.start()
        out_copies.append(cp)

    def stage_fo(chunk):
        whole((1, chunk))
        first_grad(chunk, 0, agb.at[4 + chunk])

    def stage_fp(chunk):
        u = (1, chunk)
        if chunk in F1:
            U[u, "pd", 0].wait_recv()
            if u in DIRECT_GATHER:
                U[u, "pc", 0].wait_recv()
                U[u, "pc", 1].wait_recv()
            else:
                U[u, "pd", 1].wait_recv()
        else:
            U[u, "p"].wait_recv()
        first_grad(chunk, 1, pdelta.at[chunk])

    def stage_t1():
        ready(3)
        wa[1] = wb[0].T

    def stage_t2():
        ready(2)
        wb[1] = wa[0].T

    steps = dict(
        gy=gather_y, gz=gather_z, gr=gather_relay, gl=gather_last, t1=stage_t1,
        t2=stage_t2, a=stage_a, b=stage_b, c=stage_c, d=stage_d, p=stage_p, e=stage_e,
        f=stage_f, g=stage_g, h=stage_h, sg=stage_sg, fo=stage_fo, fp=stage_fp,
        f1s=stage_f1s, f1r=stage_f1r,
    )
    for name, *args in SCHEDULE:
        steps[name](*args)
    for cp in pending:
        if id(cp) not in waited:
            cp.wait_send()
    for cp in out_copies:
        cp.wait()


def widen(lo_in, tg_in, fg_in, sg_in, lo_ref, tg_ref, fg_ref, sg_ref):
    lo_ref[...] = lo_in[...]
    tg_ref[...] = tg_in[...]
    fg_ref[...] = fg_in[...].astype(F32)
    sg_ref[...] = sg_in[...].astype(F32)


def local(tokens, first_weight, second_weight, upstream):
    vm = pl.BlockSpec(memory_space=pltpu.VMEM)
    hbm = pl.BlockSpec(memory_space=pl.ANY)
    dma = pltpu.SemaphoreType.DMA
    lo, tg, fg, sg = pl.pallas_call(
        kernel,
        out_shape=(
            jax.ShapeDtypeStruct((B, W), BF),
            jax.ShapeDtypeStruct((B, W), BF),
            jax.ShapeDtypeStruct((H, W), BF),
            jax.ShapeDtypeStruct((H, W), BF),
        ),
        in_specs=[hbm] * 4,
        out_specs=(vm, vm, hbm, hbm),
        scratch_shapes=[
            pltpu.VMEM((2, 4, C, W), BF),
            pltpu.VMEM((2, W, H), BF),
            pltpu.VMEM((2, H, W), BF),
            pltpu.VMEM((FS, C, H), F32),
            pltpu.VMEM((8, Q, H), BF),
            pltpu.VMEM((8, Q, H), BF),
            pltpu.VMEM((8, 2, Q, H), BF),
            pltpu.VMEM((8, 2, Q, H), BF),
            pltpu.VMEM((8, C, H), BF),
            pltpu.VMEM((4, Q, H), F32),
            pltpu.VMEM((4, C, H), BF),
            pltpu.VMEM((KS, 128, W), F32),
            pltpu.VMEM((SS, 128, W), BF),
            pltpu.VMEM((8, 128, W), BF),
            pltpu.VMEM((2, 3, 128, W), BF),
            pltpu.VMEM((2, 3, 128, W), BF),
            pltpu.VMEM((2, 128, W), F32),
            pltpu.VMEM((2, 3, B, W), BF),
            pltpu.VMEM((2, 3, B, W), BF),
            pltpu.VMEM((2, H, H), F32),
            dma((8,)),
            dma((2, 11)), dma((2, 11)),
            dma((8, 16)), dma((8, 16)),
            dma((2, 3)), dma((2, 3)),
        ],
        compiler_params=pltpu.CompilerParams(
            collective_id=0, has_side_effects=True, vmem_limit_bytes=60 << 20
        ),
        cost_estimate=pl.CostEstimate(
            flops=6 * 2 * 1024 * W * H, bytes_accessed=16 << 20, transcendentals=0
        ),
        name="ffn",
    )(tokens, first_weight, second_weight, upstream)
    small = pl.BlockSpec((B, W), lambda i: (0, 0))
    large = pl.BlockSpec((H // 4, W), lambda i: (i, 0))
    return pl.pallas_call(
        widen,
        grid=(4,),
        out_shape=(
            jax.ShapeDtypeStruct((B, W), BF),
            jax.ShapeDtypeStruct((B, W), BF),
            jax.ShapeDtypeStruct((H, W), F32),
            jax.ShapeDtypeStruct((H, W), F32),
        ),
        in_specs=[small, small, large, large],
        out_specs=(small, small, large, large),
        name="widen",
    )(lo, tg, fg, sg)


def solution(mesh):
    in_specs = (
        P(("col", "depth"), "row"),
        P("row", "col"),
        P("col", "row"),
        P(("col", "depth"), "row"),
    )
    out_specs = (
        P(("col", "depth"), "row"),
        P(("col", "depth"), "row"),
        P(("row", "depth"), "col"),
        P(("col", "depth"), "row"),
    )
    return jax.shard_map(local, mesh=mesh, in_specs=in_specs, out_specs=out_specs, check_vma=False)
```

time: 144 us -> 121 us (0.84); the launches traced: 142 us -> 121 us
  Pallas kernels: 132 us -> 120 us
  other arithmetic: 8.5 us -> 0 us
    pallas_call x1, Pallas kernels: 132 us -> 112 us  [local(): pl.pallas_call(kernel, out_shape=(jax.ShapeDtypeStruct((B, W), BF), jax.S...]
    convert_element_type x2 -> x0, other arithmetic: 8.5 us -> none  [local(): return (lo, tg, fg.astype(F32), sg.astype(F32))]
    pallas_call x0 -> x1, Pallas kernels: none -> 7.87 us  [local(): pl.pallas_call(widen, grid=(4,), out_shape=(jax.ShapeDtypeStruct((B, W),...]
where the time goes in v2:
time: 121 us
  Pallas kernels  120 us (99%)
    pallas_call x1, Pallas kernels, local(): pl.pallas_call(kernel, out_shape=(jax.ShapeDtypeStruct((B, W), BF), jax.S...  112 us
    pallas_call x1, Pallas kernels, local(): pl.pallas_call(widen, grid=(4,), out_shape=(jax.ShapeDtypeStruct((B, W),...  7.87 us

profile of v2, /device:TPU:1, one launch (start us, length us, event | category | flops | bytes accessed | tf_op | source)
XLA Modules:
  0.0 120.8 jit_solution(8874048600939599792)
XLA Ops:
  0.6 112.2 %ffn.1 = (bf16[32,1792]{1,0:T(8,128)(2,1)}, bf16[32,1792]{1,0:T(8,128)(2,1)}, bf16[896,1792]{1,0:T(8,128)(2,1)}, bf16[896,1792]{1,0:T(8,128)(2,1)}) custom-call(bf16[32,1792]{1,0:T(8,128)(2,1)} %tok_ref.1, bf16[1792,1792]{1,0:T(8,128)(2,1)} %w1_ref.1, bf16[1792,1792]{1,0:T(8,128)(2,1)} %w2_ref.1, bf16[32,1792]{1,0:T(8,128)(2,1)} %up_ref.1), custom_call_target="tpu_custom_call" | custom-call | flops 19730006016 | bytes 16777216 | tf_op jit(solution)/shard_map/ffn/pallas_call | solution.py:431
  112.9 7.9 %widen.1 = (bf16[32,1792]{1,0:T(8,128)(2,1)}, bf16[32,1792]{1,0:T(8,128)(2,1)}, f32[896,1792]{1,0:T(8,128)}, f32[896,1792]{1,0:T(8,128)}) custom-call(bf16[32,1792]{1,0:T(8,128)(2,1)} %get-tuple-element.8.lo_in, bf16[32,1792]{1,0:T(8,128)(2,1)} %get-tuple-element.9.tg_in, bf16[896,1792]{1,0:T(8,128)(2,1)} %get-tuple-element.10.fg_in, ...), custom_call_target="tpu_custom_call" | custom-call | tf_op jit(solution)/shard_map/widen/pallas_call | solution.py:477

commit v3 on v2

--- a/solution.py
+++ b/solution.py
@@ -18,25 +18,25 @@
 Q = 64
 B = 32
 OFFSET = (0, 1, 3, 2)
-DIRECT_SUM = ((0, 0), (1, 0))
-DIRECT_GATHER = ((1, 0), (1, 1))
-DIRECT_Z = ()
+DIRECT_SUM = ((0, 0),)
+DIRECT_GATHER = ((1, 0), (1, 2))
 FS, KS, SS = 3, 4, 4
 RELAY_Z = (0, 1)
 F1 = (0, 1, 2)
 
 SCHEDULE = (
-    ("gy", 0), ("gy", 1), ("gz", 0), ("a", 0, 0), ("gr", 0, 2), ("gr", 0, 1), ("c", 0, 0),
-    ("gz", 1), ("a", 0, 2), ("a", 0, 1), ("d", 0, 0), ("gl", 0), ("b", 0, 2), ("a", 0, 3),
-    ("b", 0, 1), ("b", 0, 3), ("t1",), ("c", 0, 2), ("t2",), ("gr", 1, 1), ("gr", 1, 2),
-    ("c", 0, 3), ("c", 0, 1), ("a", 1, 1), ("d", 0, 3), ("gl", 1), ("a", 1, 2), ("a", 1, 3),
-    ("d", 0, 2), ("e", 0, 3), ("d", 0, 1), ("b", 1, 3), ("b", 1, 2), ("f", 0, 3), ("e", 0, 2),
-    ("e", 0, 1), ("c", 1, 3), ("b", 1, 1), ("e", 0, 0), ("f", 0, 1), ("f", 0, 2), ("d", 1, 3),
-    ("c", 1, 2), ("c", 1, 1), ("p", 1, 3), ("e", 1, 3), ("d", 1, 2), ("a", 1, 0), ("f", 1, 3),
-    ("f", 0, 0), ("sg", 0), ("e", 1, 1), ("e", 1, 2), ("f1s", 1, 2), ("f", 1, 1), ("f", 1, 2),
-    ("c", 1, 0), ("fo", 3), ("sg", 1), ("f1r", 1, 2), ("f1s", 1, 0), ("g", 0), ("f1s", 1, 1),
-    ("e", 1, 0), ("fo", 1), ("f", 1, 0), ("g", 1), ("fp", 2), ("fo", 2), ("fp", 0), ("fo", 0),
-    ("fp", 3), ("fp", 1), ("h", 0), ("h", 1),
+    ("gy", 0), ("gz", 0), ("gy", 1), ("gz2", 0), ("gz1", 0), ("gz", 1), ("a", 0, 0), ("t1",),
+    ("gr", 0, 2), ("gr", 0, 1), ("a", 0, 2), ("gz1", 1), ("c", 0, 0), ("b", 0, 2), ("gl", 0),
+    ("a", 0, 1), ("a", 0, 3), ("gz2", 1), ("c", 0, 2), ("b", 0, 3), ("b", 0, 1), ("gr", 1, 1),
+    ("gr", 1, 2), ("a", 1, 1), ("c", 0, 3), ("c", 0, 1), ("t2",), ("gl", 1), ("d", 0, 3),
+    ("a", 1, 3), ("d", 0, 2), ("d", 0, 1), ("b", 1, 1), ("e", 0, 3), ("b", 1, 3), ("a", 1, 2),
+    ("f", 0, 3), ("e", 0, 1), ("c", 1, 1), ("e", 0, 2), ("c", 1, 3), ("f", 0, 2), ("b", 1, 2),
+    ("f", 0, 1), ("d", 1, 3), ("d", 1, 1), ("a", 1, 0), ("c", 1, 2), ("e", 1, 3), ("fo", 3),
+    ("f", 1, 3), ("p", 1, 3), ("b", 1, 0), ("d", 0, 0), ("f1s", 1, 1), ("e", 1, 1),
+    ("e", 1, 2), ("c", 1, 0), ("f", 1, 1), ("f", 1, 2), ("e", 0, 0), ("f", 0, 0), ("g", 0),
+    ("f1s", 1, 2), ("sg", 1), ("e", 1, 0), ("f1s", 1, 0), ("f", 1, 0), ("fo", 2), ("h", 0),
+    ("g", 1), ("f1r", 1, 1), ("fo", 0), ("sg", 0), ("fp", 2), ("fo", 1), ("fp", 0), ("fp", 3),
+    ("fp", 1), ("h", 1),
 )
 
 
@@ -113,46 +113,56 @@
     def gather_y(k):
         ready(k)
         blk = xs.at[k, z, rows(c * 128 + y * B, B)]
-        for d in (1, 3, 2):
+        for d in (2, 1, 3):
             G[k, "y", d] = send(blk, blk, *gsem(k, d - 1), dev(dy=d))
 
-    def gather_z(k):
-        for d in (1, 3, 2):
+    def forward(k, d):
+        blk = xs.at[k, z, rows(c * 128 + lax.rem(y + d, 4) * B, B)]
+        G[k, "s0", d] = send(blk, blk, *gsem(k, 3 + d), dev(dc=1))
+        G[k, "z", 1, d] = send(blk, blk, *gsem(k, 7 + d), dev(dz=1))
+        G[k, "z", 3, d] = send(blk, blk, *gsem(k, 11 + d), dev(dz=3))
+
+    def gather_z0(k):
+        forward(k, 0)
+
+    def gather_z1(k):
+        for d in (1, 3):
             G[k, "y", d].wait_recv()
-        grp = xs.at[k, z, rows(c * 128, 128)]
-        G[k, "s", 0] = send(grp, grp, *gsem(k, 3), dev(dc=1))
-        G[k, "z", 1] = send(grp, grp, *gsem(k, 4), dev(dz=1))
-        G[k, "z", 3] = send(grp, grp, *gsem(k, 5), dev(dz=3))
-        if k in DIRECT_Z:
-            G[k, "r", 1] = send(grp, grp, *gsem(k, 6), dev(dz=2))
+            forward(k, 4 - d)
+
+    def gather_z2(k):
+        G[k, "y", 2].wait_recv()
+        forward(k, 2)
 
     def gather_relay(k, chunk):
         zz = lax.rem(z + OFFSET[chunk], 4)
-        G[k, "z", 3 if chunk == 1 else 1].wait_recv()
-        if k in DIRECT_Z:
-            pass
-        elif chunk == 1:
+        for d in range(4):
+            G[k, "z", 3 if chunk == 1 else 1, d].wait_recv()
+        if chunk == 1:
             part = xs.at[k, zz, rows(c * 128 + 64, 64)]
-            G[k, "r", 1] = send(part, part, *gsem(k, 6), dev(dz=3))
+            G[k, "r", 1] = send(part, part, *gsem(k, 15), dev(dz=3))
         else:
             part = xs.at[k, zz, rows(c * 128, 64)]
-            G[k, "r", 2] = send(part, part, *gsem(k, 7), dev(dz=1))
+            G[k, "r", 2] = send(part, part, *gsem(k, 16), dev(dz=1))
         grp = xs.at[k, zz, rows(c * 128, 128)]
-        G[k, "s", chunk] = send(grp, grp, *gsem(k, 7 + chunk), dev(dc=1))
+        G[k, "s", chunk] = send(grp, grp, *gsem(k, 16 + chunk), dev(dc=1))
 
     def gather_last(k):
         G[k, "r", 1].wait_recv()
-        if k not in DIRECT_Z:
-            G[k, "r", 2].wait_recv()
+        G[k, "r", 2].wait_recv()
         grp = xs.at[k, lax.rem(z + 2, 4), rows(c * 128, 128)]
-        G[k, "s", 3] = send(grp, grp, *gsem(k, 10), dev(dc=1))
+        G[k, "s", 3] = send(grp, grp, *gsem(k, 19), dev(dc=1))
 
     grouped = set()
 
     def group(k, chunk):
         if (k, chunk) not in grouped:
             grouped.add((k, chunk))
-            G[k, "s", chunk].wait_recv()
+            if chunk == 0:
+                for d in range(4):
+                    G[k, "s0", d].wait_recv()
+            else:
+                G[k, "s", chunk].wait_recv()
 
     U = {}
     free_f, free_k, sib_sends = list(range(FS)), list(range(KS)), []
@@ -328,7 +338,7 @@
                 t = t + zr[kind, i - 1, r].astype(F32)
             return t
 
-        for d in (1, 3, 2):
+        for d in (2, 1, 3):
             ys[kind, d - 1] = total(lax.rem(y + d, 4)).astype(BF)
             U[kind, d, "y"] = send(
                 ys.at[kind, d - 1], yr.at[kind, d - 1], fsend.at[kind, d - 1],
@@ -403,7 +413,8 @@
         wb[1] = wa[0].T
 
     steps = dict(
-        gy=gather_y, gz=gather_z, gr=gather_relay, gl=gather_last, t1=stage_t1,
+        gy=gather_y, gz=gather_z0, gz1=gather_z1, gz2=gather_z2,
+        gr=gather_relay, gl=gather_last, t1=stage_t1,
         t2=stage_t2, a=stage_a, b=stage_b, c=stage_c, d=stage_d, p=stage_p, e=stage_e,
         f=stage_f, g=stage_g, h=stage_h, sg=stage_sg, fo=stage_fo, fp=stage_fp,
         f1s=stage_f1s, f1r=stage_f1r,
@@ -417,11 +428,33 @@
         cp.wait()
 
 
-def widen(lo_in, tg_in, fg_in, sg_in, lo_ref, tg_ref, fg_ref, sg_ref):
-    lo_ref[...] = lo_in[...]
-    tg_ref[...] = tg_in[...]
-    fg_ref[...] = fg_in[...].astype(F32)
-    sg_ref[...] = sg_in[...].astype(F32)
+def widen(
+    lo_in, tg_in, fg_in, sg_in, lo_ref, tg_ref, fg_ref, sg_ref,
+    narrow, wide, small_sem, in_sem, out_sem,
+):
+    small = [
+        pltpu.make_async_copy(lo_in, lo_ref, small_sem.at[0]),
+        pltpu.make_async_copy(tg_in, tg_ref, small_sem.at[1]),
+    ]
+    ins, outs = [], []
+    size = H // 4
+    for i in range(4):
+        for a, src in enumerate((fg_in, sg_in)):
+            r = slice(i * size, i * size + size)
+            cp = pltpu.make_async_copy(src.at[r], narrow.at[a, r], in_sem.at[a, i])
+            cp.start()
+            ins.append((a, i, r, cp))
+    for cp in small:
+        cp.start()
+    for a, i, r, cp in ins:
+        cp.wait()
+        wide[a, r] = narrow[a, r].astype(F32)
+        dst = (fg_ref, sg_ref)[a]
+        out = pltpu.make_async_copy(wide.at[a, r], dst.at[r], out_sem.at[a, i])
+        out.start()
+        outs.append(out)
+    for cp in outs + small:
+        cp.wait()
 
 
 def local(tokens, first_weight, second_weight, upstream):
@@ -460,7 +493,7 @@
             pltpu.VMEM((2, 3, B, W), BF),
             pltpu.VMEM((2, H, H), F32),
             dma((8,)),
-            dma((2, 11)), dma((2, 11)),
+            dma((2, 20)), dma((2, 20)),
             dma((8, 16)), dma((8, 16)),
             dma((2, 3)), dma((2, 3)),
         ],
@@ -472,19 +505,21 @@
         ),
         name="ffn",
     )(tokens, first_weight, second_weight, upstream)
-    small = pl.BlockSpec((B, W), lambda i: (0, 0))
-    large = pl.BlockSpec((H // 4, W), lambda i: (i, 0))
     return pl.pallas_call(
         widen,
-        grid=(4,),
         out_shape=(
             jax.ShapeDtypeStruct((B, W), BF),
             jax.ShapeDtypeStruct((B, W), BF),
             jax.ShapeDtypeStruct((H, W), F32),
             jax.ShapeDtypeStruct((H, W), F32),
         ),
-        in_specs=[small, small, large, large],
-        out_specs=(small, small, large, large),
+        in_specs=[hbm] * 4,
+        out_specs=(hbm,) * 4,
+        scratch_shapes=[
+            pltpu.VMEM((2, H, W), BF), pltpu.VMEM((2, H, W), F32),
+            dma((2,)), dma((2, 4)), dma((2, 4)),
+        ],
+        compiler_params=pltpu.CompilerParams(vmem_limit_bytes=40 << 20),
         name="widen",
     )(lo, tg, fg, sg)
 

time: 121 us -> 124 us (1.025)
  local copies, waits for them, and re-layouts: 0 us -> 5.6 us
  Pallas kernels: 120 us -> 117 us
    unnamed x0 -> x8, local copies, waits for them, and re-layouts: none -> 5.6 us
    pallas_call x1, Pallas kernels: 7.87 us -> 5.53 us  [local(): pl.pallas_call(widen, out_shape=(jax.ShapeDtypeStruct((B, W), BF), jax.Sh...]
where the time goes in v3:
time: 124 us
  Pallas kernels  117 us (94%)
  local copies, waits for them, and re-layouts  5.6 us (5%)
    pallas_call x1, Pallas kernels, local(): pl.pallas_call(kernel, out_shape=(jax.ShapeDtypeStruct((B, W), BF), jax.S...  112 us
    unnamed x8, local copies, waits for them, and re-layouts  5.6 us
    pallas_call x1, Pallas kernels, local(): pl.pallas_call(widen, out_shape=(jax.ShapeDtypeStruct((B, W), BF), jax.Sh...  5.53 us

profile of v3, /device:TPU:1, one launch (start us, length us, event | category | flops | bytes accessed | tf_op | source)
XLA Modules:
  0.0 123.7 jit_solution(10529283108209259126)
XLA Ops:
  0.6 111.8 %ffn.1 = (bf16[32,1792]{1,0:T(8,128)(2,1)}, bf16[32,1792]{1,0:T(8,128)(2,1)}, bf16[896,1792]{1,0:T(8,128)(2,1)}, bf16[896,1792]{1,0:T(8,128)(2,1)}) custom-call(bf16[32,1792]{1,0:T(8,128)(2,1)} %tok_ref.1, bf16[1792,1792]{1,0:T(8,128)(2,1)} %w1_ref.1, bf16[1792,1792]{1,0:T(8,128)(2,1)} %w2_ref.1, bf16[32,1792]{1,0:T(8,128)(2,1)} %up_ref.1), custom_call_target="tpu_custom_call" | custom-call | flops 19730006016 | bytes 16777216 | tf_op jit(solution)/shard_map/ffn/pallas_call | solution.py:464
  112.4 0.0 copy-start
  112.4 1.9 %copy-done = bf16[896,1792]{1,0:T(8,128)(2,1)S(1)} copy-done((bf16[896,1792]{1,0:T(8,128)(2,1)S(1)}, bf16[896,1792]{1,0:T(8,128)(2,1)}, u32[]{:S(2)}) %copy-start) | copy-done | bytes 3211288
  114.3 0.0 copy-start.1
  114.3 1.9 %copy-done.1 = bf16[896,1792]{1,0:T(8,128)(2,1)S(1)} copy-done((bf16[896,1792]{1,0:T(8,128)(2,1)S(1)}, bf16[896,1792]{1,0:T(8,128)(2,1)}, u32[]{:S(2)}) %copy-start.1) | copy-done | bytes 3211288
  116.2 0.0 copy-start.2
  116.2 0.9 copy-done.2
  117.1 0.0 copy-start.3
  117.1 0.9 copy-done.3
  118.0 5.5 %widen.1 = (bf16[32,1792]{1,0:T(8,128)(2,1)}, bf16[32,1792]{1,0:T(8,128)(2,1)}, f32[896,1792]{1,0:T(8,128)}, f32[896,1792]{1,0:T(8,128)}) custom-call(bf16[32,1792]{1,0:T(8,128)(2,1)S(1)} %copy-done.2, bf16[32,1792]{1,0:T(8,128)(2,1)S(1)} %copy-done.3, bf16[896,1792]{1,0:T(8,128)(2,1)S(1)} %copy-done, bf16[896,1792]{1,0:T(8,128)(2,1)S(1)} %copy-done.1), custom_call_target="tpu_custom_call" | custom-call | tf_op jit(solution)/shard_map/widen/pallas_call | solution.py:508
Async XLA Ops:
  112.4 1.9 %copy-start = (bf16[896,1792]{1,0:T(8,128)(2,1)S(1)}, bf16[896,1792]{1,0:T(8,128)(2,1)}, u32[]{:S(2)}) copy-start(bf16[896,1792]{1,0:T(8,128)(2,1)} %get-tuple-element.10.fg_in) | copy-start | bytes 9633796
  114.3 1.9 %copy-start.1 = (bf16[896,1792]{1,0:T(8,128)(2,1)S(1)}, bf16[896,1792]{1,0:T(8,128)(2,1)}, u32[]{:S(2)}) copy-start(bf16[896,1792]{1,0:T(8,128)(2,1)} %get-tuple-element.11.sg_in) | copy-start | bytes 9633796
  116.2 0.9 copy-start.2
  117.1 0.9 copy-start.3

commit v4 on v3

v4 whole, which is shorter than its diff:
```python
import math

import jax
import jax.numpy as jnp
from jax import lax
from jax.experimental import pallas as pl
from jax.experimental.pallas import tpu as pltpu
from jax.sharding import PartitionSpec as P

MESH = pl.DeviceIdType.MESH
BF = jnp.bfloat16
F32 = jnp.float32
SCALE = math.sqrt(2.0 / math.pi)

W = 1792
H = 896
C = 256
Q = 64
B = 32
OFFSET = (0, 1, 3, 2)
DIRECT_SUM = ((0, 0), (0, 4), (1, 0), (1, 4))
DIRECT_GATHER = ((1, 1), (1, 2), (1, 4))
FS, KS, SS = 4, 4, 4
RELAY_Z = (1,)
F1 = (1, 2, 4)

SCHEDULE = (
    ("gy", 0), ("t1",), ("gz", 0), ("gz1", 0), ("gy", 1), ("a", 0, 0), ("gz2", 0), ("gz", 1),
    ("a", 0, 4), ("gz1", 1), ("a", 1, 0), ("gr", 0, 2), ("c", 0, 0), ("gr", 0, 1),
    ("c", 0, 4), ("gz2", 1), ("a", 0, 2), ("c", 1, 0), ("a", 0, 1), ("b", 0, 2), ("d", 0, 0),
    ("b", 0, 1), ("gl", 0), ("c", 0, 2), ("a", 0, 3), ("gr", 1, 1), ("c", 0, 1), ("gr", 1, 2),
    ("d", 0, 2), ("a", 1, 1), ("b", 0, 3), ("d", 0, 1), ("a", 1, 2), ("gl", 1), ("e", 0, 2),
    ("a", 1, 3), ("c", 0, 3), ("e", 0, 1), ("f", 0, 2), ("b", 1, 3), ("f", 0, 1), ("t2",),
    ("d", 0, 3), ("b", 1, 2), ("e", 0, 0), ("c", 1, 3), ("e", 0, 3), ("b", 1, 1), ("f", 0, 3),
    ("d", 1, 3), ("c", 1, 2), ("c", 1, 1), ("d", 1, 0), ("f", 0, 0), ("d", 0, 4), ("a", 1, 4),
    ("e", 1, 3), ("p", 1, 3), ("f", 1, 3), ("e", 1, 2), ("e", 1, 1), ("f1s", 1, 1),
    ("e", 0, 4), ("f", 1, 2), ("p", 1, 0), ("f", 1, 1), ("sg", 0), ("f", 0, 4), ("c", 1, 4),
    ("g", 0, 0), ("e", 1, 0), ("fo", 2), ("g", 0, 4), ("f1s", 1, 2), ("fo", 1), ("f", 1, 0),
    ("fp", 1), ("e", 1, 4), ("f1s", 1, 4), ("fo", 0), ("fp", 0), ("f", 1, 4), ("fp", 3),
    ("g", 1, 4), ("g", 1, 0), ("sg", 1), ("fp", 2), ("fo", 3), ("h", 0), ("fo", 4), ("fp", 4),
    ("h", 1),
)


def gelu_and_slope(h):
    inner = SCALE * (h + 0.044715 * h * h * h)
    t = jnp.tanh(inner)
    value = 0.5 * h * (1.0 + t)
    slope = 0.5 * (1.0 + t) + 0.5 * h * (1.0 - t * t) * SCALE * (
        1.0 + 3.0 * 0.044715 * h * h
    )
    return value, slope


def kernel(
    tok_ref, w1_ref, w2_ref, up_ref,
    lo_ref, tg_ref, fg_ref, sg_ref,
    xs, wa, wb, hp, rs1s, rs1r, rs2s, rs2r, agb, slope, pdelta,
    keep, sibs, sibr, zr, s0, ys, yr, facc,
    lsem, gsend, grecv, usend, urecv, fsend, frecv,
):
    x = lax.axis_index("row")
    col = lax.axis_index("col")
    yh = lax.axis_index("depth")
    z, yl, c = col // 4, (col // 2) % 2, col % 2
    y = yh * 2 + yl

    def dev(dx=0, dy=0, dz=0, dc=0):
        xx, yy = lax.rem(x + dx, 4), lax.rem(y + dy, 4)
        zz, cc = lax.rem(z + dz, 4), lax.rem(c + dc, 2)
        return (xx, zz * 4 + lax.rem(yy, 2) * 2 + cc, yy // 2)

    pending, waited = [], []

    def send(src, dst, ss, rs, to):
        cp = pltpu.make_async_remote_copy(
            src_ref=src, dst_ref=dst, send_sem=ss, recv_sem=rs,
            device_id=to, device_id_type=MESH,
        )
        cp.start()
        pending.append(cp)
        return cp

    def rows(start, size):
        return pl.ds(pl.multiple_of(start, size), size)

    half = rows(yh * H, H)
    in_copies = [
        pltpu.make_async_copy(tok_ref, xs.at[0, z, rows(c * 128 + y * B, B)], lsem.at[0]),
        pltpu.make_async_copy(up_ref, xs.at[1, z, rows(c * 128 + y * B, B)], lsem.at[1]),
        pltpu.make_async_copy(w1_ref.at[:, half], wa.at[0], lsem.at[2]),
        pltpu.make_async_copy(w2_ref.at[half, :], wb.at[0], lsem.at[3]),
    ]
    for cp in in_copies:
        cp.start()
    loaded = set()

    def ready(i):
        if i not in loaded:
            loaded.add(i)
            in_copies[i].wait()

    barrier = pltpu.get_barrier_semaphore()
    peers = [dev(dc=1), dev(dx=1), dev(dx=2), dev(dx=3), dev(dy=1), dev(dy=2), dev(dy=3),
             dev(dz=1), dev(dz=2), dev(dz=3)]
    for p in peers:
        pl.semaphore_signal(barrier, inc=1, device_id=p, device_id_type=MESH)
    pl.semaphore_wait(barrier, len(peers))

    G = {}

    def gsem(k, i):
        return gsend.at[k, i], grecv.at[k, i]

    SHIFT = (0, 1 + 2 * yl, 2, 3 - 2 * yl)

    def gather_y(k):
        ready(k)
        blk = xs.at[k, z, rows(c * 128 + y * B, B)]
        for d in (1, 3, 2):
            G[k, "y", d] = send(blk, blk, *gsem(k, d - 1), dev(dy=SHIFT[d]))

    def forward(k, d):
        blk = xs.at[k, z, rows(c * 128 + lax.rem(y + SHIFT[d], 4) * B, B)]
        G[k, "s0", d] = send(blk, blk, *gsem(k, 3 + d), dev(dc=1))
        G[k, "z", 1, d] = send(blk, blk, *gsem(k, 7 + d), dev(dz=1))
        G[k, "z", 3, d] = send(blk, blk, *gsem(k, 11 + d), dev(dz=3))

    def gather_z0(k):
        forward(k, 0)

    def gather_z1(k):
        G[k, "y", 1].wait_recv()
        forward(k, 1)

    def gather_z2(k):
        for d in (3, 2):
            G[k, "y", d].wait_recv()
            forward(k, d)

    def gather_relay(k, chunk):
        zz = lax.rem(z + OFFSET[chunk], 4)
        for d in range(4):
            G[k, "z", 3 if chunk == 1 else 1, d].wait_recv()
        if chunk == 1:
            part = xs.at[k, zz, rows(c * 128 + 64, 64)]
            G[k, "r", 1] = send(part, part, *gsem(k, 15), dev(dz=3))
        else:
            part = xs.at[k, zz, rows(c * 128, 64)]
            G[k, "r", 2] = send(part, part, *gsem(k, 16), dev(dz=1))
        grp = xs.at[k, zz, rows(c * 128, 128)]
        G[k, "s", chunk] = send(grp, grp, *gsem(k, 16 + chunk), dev(dc=1))

    def gather_last(k):
        G[k, "r", 1].wait_recv()
        G[k, "r", 2].wait_recv()
        grp = xs.at[k, lax.rem(z + 2, 4), rows(c * 128, 128)]
        G[k, "s", 3] = send(grp, grp, *gsem(k, 19), dev(dc=1))

    grouped = set()

    def group(k, chunk):
        if (k, chunk) not in grouped:
            grouped.add((k, chunk))
            if chunk in (0, 4):
                for d in ((0, 1) if chunk == 0 else (3, 2)):
                    G[k, "s0", d].wait_recv()
            else:
                G[k, "s", chunk].wait_recv()

    U = {}
    free_f, free_k, sib_sends = list(range(FS)), list(range(KS)), []
    slot_f, slot_k = {}, {}

    def usem(u, i):
        n = u[0] * 5 + u[1]
        return usend.at[n, i], urecv.at[n, i]

    def size(u):
        return C // 2 if u[1] in (0, 4) else C

    def buf(ref, u, part=1, lead=()):
        m = size(u) // part
        start = m if u[1] == 4 else 0
        return ref.at[(u[0] * 4 + u[1] % 4,) + lead + (slice(start, start + m),)]

    def pd(u):
        return buf(pdelta, (0, u[1]))

    def tokens(k, chunk, other=False, lanes=slice(None)):
        if chunk in (0, 4):
            h = yh if (chunk == 0) != other else 1 - yh
            return jnp.concatenate(
                [xs[k, z, rows(cc * 128 + h * 64, 64), lanes] for cc in (0, 1)], axis=0
            )
        return xs[k, lax.rem(z + OFFSET[chunk], 4), :, lanes]

    def stage_a(*u):
        kind, chunk = u
        group(kind, chunk)
        if kind == 0:
            ready(2)
        q = size(u) // 4
        e = q // 2
        f = hp.at[slot_f.setdefault(u, free_f.pop(0)), 0 : size(u)]
        f[...] = jnp.dot(tokens(kind, chunk), wa[kind], preferred_element_type=F32)
        away, into = buf(rs1s, u, 4), buf(rs1r, u, 4)
        away[...] = f[rows(lax.rem(x + 2, 4) * q, q)].astype(BF)
        if u in DIRECT_SUM:
            U[u, "a", 0] = send(away, into, *usem(u, 0), dev(dx=2))
            for i, d in enumerate((1, 3)):
                out, into = buf(rs2s, u, 4, (i,)), buf(rs2r, u, 4, (i,))
                out[...] = f[rows(lax.rem(x + d, 4) * q, q)].astype(BF)
                U[u, "b", i] = send(out, into, *usem(u, 2 + i), dev(dx=d))
            return
        U[u, "a", 0] = send(away.at[0:e], into.at[0:e], *usem(u, 0), dev(dx=1))
        U[u, "a", 1] = send(away.at[e:q], into.at[e:q], *usem(u, 1), dev(dx=3))

    def stage_b(*u):
        q = size(u) // 4
        e = q // 2
        f, got = hp.at[slot_f[u], 0 : size(u)], buf(rs1r, u, 4)
        for i, d in enumerate((1, 3)):
            out, into = buf(rs2s, u, 4, (i,)), buf(rs2r, u, 4, (i,))
            start = lax.rem(x + d, 4) * q
            r, o = (slice(0, e), slice(e, q))[:: 1 - 2 * i]
            U[u, "a", i].wait_recv()
            out[r] = (f[rows(start + i * e, e)] + got[r].astype(F32)).astype(BF)
            out[o] = f[rows(start + e - i * e, e)].astype(BF)
            U[u, "b", i] = send(out, into, *usem(u, 2 + i), dev(dx=d))

    def stage_c(*u):
        kind, chunk = u
        q = size(u) // 4
        f, ag = hp.at[slot_f[u], 0 : size(u)], buf(agb, u)
        right, left = buf(rs2r, u, 4, (0,)), buf(rs2r, u, 4, (1,))
        sl_ref = buf(slope, (0, chunk), 4)
        U[u, "b", 0].wait_recv()
        U[u, "b", 1].wait_recv()
        if u in DIRECT_SUM:
            U[u, "a", 0].wait_recv()
        for n in range(0, q, 32):
            r = slice(n, n + 32)
            h = f[rows(x * q + n, 32)] + right[r].astype(F32) + left[r].astype(F32)
            if u in DIRECT_SUM:
                h = h + buf(rs1r, u, 4)[r].astype(F32)
            if kind == 0:
                value, sl = gelu_and_slope(h)
                sl_ref[r] = sl
            else:
                value = h * sl_ref[r]
            ag[rows(x * q + n, 32)] = value.astype(BF)
        free_f.append(slot_f[u])
        mine = ag.at[rows(x * q, q)]
        if kind == 1 and chunk in F1:
            U[u, "p"] = send(mine, pd(u).at[rows(x * q, q)], *usem(u, 8), dev(dy=2))
        if u in DIRECT_GATHER:
            U[u, "d", 0] = send(mine, mine, *usem(u, 6), dev(dx=2))
        U[u, "c", 0] = send(mine, mine, *usem(u, 4), dev(dx=1))
        U[u, "c", 1] = send(mine, mine, *usem(u, 5), dev(dx=3))

    def pass_on(u, ref, first, then, sem):
        q = size(u) // 4
        e = q // 2
        U[u, first, 0].wait_recv()
        part = ref.at[rows(lax.rem(x + 3, 4) * q, e)]
        U[u, then, 0] = send(part, part, *usem(u, sem), dev(dx=1))
        U[u, first, 1].wait_recv()
        part = ref.at[rows(lax.rem(x + 1, 4) * q + e, e)]
        U[u, then, 1] = send(part, part, *usem(u, sem + 1), dev(dx=3))

    def stage_d(*u):
        pass_on(u, buf(agb, u), "c", "d", 6)

    def stage_f1s(*u):
        q = size(u) // 4
        part = pd(u).at[rows(x * q, q)]
        U[u, "p"].wait_recv()
        if u in DIRECT_GATHER:
            U[u, "pd", 0] = send(part, part, *usem(u, 14), dev(dx=2))
        U[u, "pc", 0] = send(part, part, *usem(u, 12), dev(dx=1))
        U[u, "pc", 1] = send(part, part, *usem(u, 13), dev(dx=3))

    def stage_f1r(*u):
        pass_on(u, pd(u), "pc", "pd", 14)

    gathered = set()

    def whole(u):
        if u not in gathered:
            gathered.add(u)
            U[u, "d", 0].wait_recv()
            if u in DIRECT_GATHER:
                U[u, "c", 0].wait_recv()
                U[u, "c", 1].wait_recv()
            else:
                U[u, "d", 1].wait_recv()

    def stage_p(*u):
        whole(u)
        U[u, "p"] = send(buf(agb, u), pd(u), *usem(u, 8), dev(dy=2))

    def stage_e(*u):
        kind = u[0]
        whole(u)
        if kind == 0:
            ready(3)
        n = len(sib_sends)
        if n >= SS:
            sib_sends[n - SS].wait_send()
            waited.append(id(sib_sends[n - SS]))
        m = size(u) // 2
        out = sibs.at[n % SS, 0:m]
        k = keep.at[slot_k.setdefault(u, free_k.pop(0)), 0:m]
        ag = buf(agb, u)
        lhs = jnp.concatenate([ag[rows((1 - c) * m, m)], ag[rows(c * m, m)]], axis=0)
        part = jnp.dot(lhs, wb[kind], preferred_element_type=F32)
        out[...] = part[:m].astype(BF)
        U[u, "e"] = send(out, buf(sibr, u, 2), *usem(u, 9), dev(dc=1))
        k[...] = part[m:]
        sib_sends.append(U[u, "e"])

    def stage_f(*u):
        kind, chunk = u
        U[u, "e"].wait_recv()
        m = size(u) // 2
        k, got = keep.at[slot_k[u], 0:m], buf(sibr, u, 2)
        relayed = kind in RELAY_Z and chunk in (1, 2)
        if relayed:
            U[kind, chunk, "zr"].wait_recv()
        for n in range(m // B):
            r = slice(n * B, n * B + B)
            total = k[r] + got[r].astype(F32)
            if relayed and n // 2 == chunk - 1:
                total = total + zr[kind, 2, r].astype(F32)
            if chunk in (0, 4):
                h = yh if chunk == 0 else 1 - yh
                s0[kind, rows(h * 64 + n * B, B)] = total
            else:
                got[r] = total.astype(BF)
        free_k.append(slot_k[u])
        if kind in RELAY_Z and chunk == 3:
            for i, d in ((1, 1), (2, 3)):
                r = slice(i * 64 - 64, i * 64)
                U[kind, i, "zr"] = send(
                    got.at[r], zr.at[kind, 2, r], *usem((kind, i), 11), dev(dz=d)
                )
        elif chunk not in (0, 4):
            U[kind, chunk, "z"] = send(
                got, zr.at[kind, chunk - 1], *usem(u, 10),
                dev(dz=OFFSET[chunk]),
            )

    z_done = set()

    def stage_g(kind, chunk):
        parts = (1, 2) if kind in RELAY_Z else (1, 2, 3)
        if kind not in z_done:
            z_done.add(kind)
            for i in parts:
                U[kind, i, "z"].wait_recv()

        def total(blk):
            r = rows(blk * B, B)
            t = s0[kind, r]
            for i in parts:
                t = t + zr[kind, i - 1, r].astype(F32)
            return t

        for d in (1,) if chunk == 0 else (2, 3):
            ys[kind, d - 1] = total(lax.rem(y + SHIFT[d], 4)).astype(BF)
            U[kind, d, "y"] = send(
                ys.at[kind, d - 1], yr.at[kind, d - 1], fsend.at[kind, d - 1],
                frecv.at[kind, d - 1], dev(dy=SHIFT[d]),
            )
        if chunk == 0:
            s0[kind, rows(y * B, B)] = total(y)

    def stage_h(kind):
        t = s0[kind, rows(y * B, B)]
        for d in (3, 2, 1):
            U[kind, d, "y"].wait_recv()
            t = t + yr[kind, d - 1].astype(F32)
        (lo_ref, tg_ref)[kind][...] = t.astype(BF)

    count = [0, 0]

    def lead(a, b):
        return lax.dot_general(a, b, (((0,), (0,)), ((), ())), preferred_element_type=F32)

    def stage_sg(part):
        at = slice(part * H, part * H + H)
        t = None
        for j in range(5):
            whole((0, j))
            group(1, j)
        for j in range(4):
            right = tokens(1, j, lanes=at)
            if j == 0:
                right = jnp.concatenate([right, tokens(1, 4, lanes=at)], axis=0)
            p = lead(agb[j], right)
            t = p if t is None else t + p
        sg_ref[:, at] = t.astype(BF)

    def first_grad(chunk, side, src):
        p = lead(tokens(0, chunk, side == 1, half), src[...])
        if count[side]:
            p = p + facc[side]
        count[side] += 1
        if count[side] < 5:
            facc[side] = p
            return
        fg_ref[:, rows((1 - yh if side else yh) * H, H)] = p.astype(BF)

    def stage_fo(chunk):
        whole((1, chunk))
        first_grad(chunk, 0, buf(agb, (1, chunk)))

    def stage_fp(chunk):
        u = (1, chunk)
        if chunk in F1:
            U[u, "pd", 0].wait_recv()
            if u in DIRECT_GATHER:
                U[u, "pc", 0].wait_recv()
                U[u, "pc", 1].wait_recv()
            else:
                U[u, "pd", 1].wait_recv()
        else:
            U[u, "p"].wait_recv()
        first_grad(chunk, 1, pd(u))

    def stage_t1():
        ready(3)
        wa[1] = wb[0].T

    def stage_t2():
        ready(2)
        wb[1] = wa[0].T

    steps = dict(
        gy=gather_y, gz=gather_z0, gz1=gather_z1, gz2=gather_z2,
        gr=gather_relay, gl=gather_last, t1=stage_t1,
        t2=stage_t2, a=stage_a, b=stage_b, c=stage_c, d=stage_d, p=stage_p, e=stage_e,
        f=stage_f, g=stage_g, h=stage_h, sg=stage_sg, fo=stage_fo, fp=stage_fp,
        f1s=stage_f1s, f1r=stage_f1r,
    )
    for name, *args in SCHEDULE:
        steps[name](*args)
    for cp in pending:
        if id(cp) not in waited:
            cp.wait_send()


def widen(lo_in, tg_in, fg_in, sg_in, lo_ref, tg_ref, fg_ref, sg_ref, wide, sem):
    copies = []
    size = H // 4
    for i in range(4):
        for a, (src, dst) in enumerate(((fg_in, fg_ref), (sg_in, sg_ref))):
            r = slice(i * size, i * size + size)
            wide[a, r] = src[r].astype(F32)
            cp = pltpu.make_async_copy(wide.at[a, r], dst.at[r], sem.at[a, i])
            cp.start()
            copies.append(cp)
    lo_ref[...] = lo_in[...]
    tg_ref[...] = tg_in[...]
    for cp in copies:
        cp.wait()


def local(tokens, first_weight, second_weight, upstream):
    vm = pl.BlockSpec(memory_space=pltpu.VMEM)
    hbm = pl.BlockSpec(memory_space=pl.ANY)
    dma = pltpu.SemaphoreType.DMA
    lo, tg, fg, sg = pl.pallas_call(
        kernel,
        out_shape=(
            pltpu.VMEM((B, W), BF),
            pltpu.VMEM((B, W), BF),
            pltpu.VMEM((H, W), BF),
            pltpu.VMEM((H, W), BF),
        ),
        in_specs=[hbm] * 4,
        out_specs=(vm,) * 4,
        scratch_shapes=[
            pltpu.VMEM((2, 4, C, W), BF),
            pltpu.VMEM((2, W, H), BF),
            pltpu.VMEM((2, H, W), BF),
            pltpu.VMEM((FS, C, H), F32),
            pltpu.VMEM((8, Q, H), BF),
            pltpu.VMEM((8, Q, H), BF),
            pltpu.VMEM((8, 2, Q, H), BF),
            pltpu.VMEM((8, 2, Q, H), BF),
            pltpu.VMEM((8, C, H), BF),
            pltpu.VMEM((4, Q, H), F32),
            pltpu.VMEM((4, C, H), BF),
            pltpu.VMEM((KS, 128, W), F32),
            pltpu.VMEM((SS, 128, W), BF),
            pltpu.VMEM((8, 128, W), BF),
            pltpu.VMEM((2, 3, 128, W), BF),
            pltpu.VMEM((2, 128, W), F32),
            pltpu.VMEM((2, 3, B, W), BF),
            pltpu.VMEM((2, 3, B, W), BF),
            pltpu.VMEM((2, H, H), F32),
            dma((4,)),
            dma((2, 20)), dma((2, 20)),
            dma((10, 16)), dma((10, 16)),
            dma((2, 3)), dma((2, 3)),
        ],
        compiler_params=pltpu.CompilerParams(
            collective_id=0, has_side_effects=True, vmem_limit_bytes=57 << 20
        ),
        cost_estimate=pl.CostEstimate(
            flops=6 * 2 * 1024 * W * H, bytes_accessed=16 << 20, transcendentals=0
        ),
        name="ffn",
    )(tokens, first_weight, second_weight, upstream)
    return pl.pallas_call(
        widen,
        out_shape=(
            jax.ShapeDtypeStruct((B, W), BF),
            jax.ShapeDtypeStruct((B, W), BF),
            jax.ShapeDtypeStruct((H, W), F32),
            jax.ShapeDtypeStruct((H, W), F32),
        ),
        in_specs=[vm] * 4,
        out_specs=(vm, vm, hbm, hbm),
        scratch_shapes=[pltpu.VMEM((2, H, W), F32), dma((2, 4))],
        compiler_params=pltpu.CompilerParams(vmem_limit_bytes=40 << 20),
        name="widen",
    )(lo, tg, fg, sg)


def solution(mesh):
    in_specs = (
        P(("col", "depth"), "row"),
        P("row", "col"),
        P("col", "row"),
        P(("col", "depth"), "row"),
    )
    out_specs = (
        P(("col", "depth"), "row"),
        P(("col", "depth"), "row"),
        P(("row", "depth"), "col"),
        P(("col", "depth"), "row"),
    )
    return jax.shard_map(local, mesh=mesh, in_specs=in_specs, out_specs=out_specs, check_vma=False)
```

time: 124 us -> 109 us (0.88)
  Pallas kernels: 117 us -> 108 us
  local copies, waits for them, and re-layouts: 5.6 us -> 0 us
    pallas_call x1, Pallas kernels: 112 us -> 103 us  [local(): pl.pallas_call(kernel, out_shape=(pltpu.VMEM((B, W), BF), pltpu.VMEM((B,...]
    unnamed x8 -> x0, local copies, waits for them, and re-layouts: 5.6 us -> none
where the time goes in v4:
time: 109 us
  Pallas kernels  108 us (99%)
    pallas_call x1, Pallas kernels, local(): pl.pallas_call(kernel, out_shape=(pltpu.VMEM((B, W), BF), pltpu.VMEM((B,...  103 us
    pallas_call x1, Pallas kernels, local(): pl.pallas_call(widen, out_shape=(jax.ShapeDtypeStruct((B, W), BF), jax.Sh...  5.53 us

profile of v4, /device:TPU:1, one launch (start us, length us, event | category | flops | bytes accessed | tf_op | source)
XLA Modules:
  0.0 109.3 jit_solution(17804804457472801491)
XLA Ops:
  0.6 103.0 %ffn.1 = (bf16[32,1792]{1,0:T(8,128)(2,1)S(1)}, bf16[32,1792]{1,0:T(8,128)(2,1)S(1)}, bf16[896,1792]{1,0:T(8,128)(2,1)S(1)}, bf16[896,1792]{1,0:T(8,128)(2,1)S(1)}) custom-call(bf16[32,1792]{1,0:T(8,128)(2,1)} %tok_ref.1, bf16[1792,1792]{1,0:T(8,128)(2,1)} %w1_ref.1, bf16[1792,1792]{1,0:T(8,128)(2,1)} %w2_ref.1, bf16[32,1792]{1,0:T(8,128)(2,1)} %up_ref.1), custom_call_target="tpu_custom_call" | custom-call | flops 19730006016 | bytes 16777216 | tf_op jit(solution)/shard_map/ffn/pallas_call | solution.py:474
  103.6 5.5 %widen.1 = (bf16[32,1792]{1,0:T(8,128)(2,1)}, bf16[32,1792]{1,0:T(8,128)(2,1)}, f32[896,1792]{1,0:T(8,128)}, f32[896,1792]{1,0:T(8,128)}) custom-call(bf16[32,1792]{1,0:T(8,128)(2,1)S(1)} %get-tuple-element.8.lo_in, bf16[32,1792]{1,0:T(8,128)(2,1)S(1)} %get-tuple-element.9.tg_in, bf16[896,1792]{1,0:T(8,128)(2,1)S(1)} %get-tuple-element.10.fg_in, ...), custom_call_target="tpu_custom_call" | custom-call | tf_op jit(solution)/shard_map/widen/pallas_call | solution.py:517

commit v5 on v4

--- a/solution.py
+++ b/solution.py
@@ -18,27 +18,27 @@
 Q = 64
 B = 32
 OFFSET = (0, 1, 3, 2)
-DIRECT_SUM = ((0, 0), (0, 4), (1, 0), (1, 4))
-DIRECT_GATHER = ((1, 1), (1, 2), (1, 4))
-FS, KS, SS = 4, 4, 4
+DIRECT_SUM = ((0, 0), (0, 4), (1, 0))
+DIRECT_GATHER = ((1, 1), (1, 4))
+FS, KS, SS = 4, 3, 3
 RELAY_Z = (1,)
 F1 = (1, 2, 4)
 
 SCHEDULE = (
-    ("gy", 0), ("t1",), ("gz", 0), ("gz1", 0), ("gy", 1), ("a", 0, 0), ("gz2", 0), ("gz", 1),
-    ("a", 0, 4), ("gz1", 1), ("a", 1, 0), ("gr", 0, 2), ("c", 0, 0), ("gr", 0, 1),
-    ("c", 0, 4), ("gz2", 1), ("a", 0, 2), ("c", 1, 0), ("a", 0, 1), ("b", 0, 2), ("d", 0, 0),
-    ("b", 0, 1), ("gl", 0), ("c", 0, 2), ("a", 0, 3), ("gr", 1, 1), ("c", 0, 1), ("gr", 1, 2),
-    ("d", 0, 2), ("a", 1, 1), ("b", 0, 3), ("d", 0, 1), ("a", 1, 2), ("gl", 1), ("e", 0, 2),
-    ("a", 1, 3), ("c", 0, 3), ("e", 0, 1), ("f", 0, 2), ("b", 1, 3), ("f", 0, 1), ("t2",),
-    ("d", 0, 3), ("b", 1, 2), ("e", 0, 0), ("c", 1, 3), ("e", 0, 3), ("b", 1, 1), ("f", 0, 3),
-    ("d", 1, 3), ("c", 1, 2), ("c", 1, 1), ("d", 1, 0), ("f", 0, 0), ("d", 0, 4), ("a", 1, 4),
-    ("e", 1, 3), ("p", 1, 3), ("f", 1, 3), ("e", 1, 2), ("e", 1, 1), ("f1s", 1, 1),
-    ("e", 0, 4), ("f", 1, 2), ("p", 1, 0), ("f", 1, 1), ("sg", 0), ("f", 0, 4), ("c", 1, 4),
-    ("g", 0, 0), ("e", 1, 0), ("fo", 2), ("g", 0, 4), ("f1s", 1, 2), ("fo", 1), ("f", 1, 0),
-    ("fp", 1), ("e", 1, 4), ("f1s", 1, 4), ("fo", 0), ("fp", 0), ("f", 1, 4), ("fp", 3),
-    ("g", 1, 4), ("g", 1, 0), ("sg", 1), ("fp", 2), ("fo", 3), ("h", 0), ("fo", 4), ("fp", 4),
-    ("h", 1),
+    ("gy", 0), ("gz", 0), ("gz1", 0), ("gy", 1), ("a", 0, 0), ("gz2", 0), ("a", 0, 4),
+    ("t1",), ("gz", 1), ("gz1", 1), ("c", 0, 0), ("a", 1, 0), ("gz2", 1), ("gr", 0, 1),
+    ("c", 0, 4), ("a", 1, 4), ("gr", 0, 2), ("a", 0, 1), ("c", 1, 0), ("a", 0, 2),
+    ("b", 0, 1), ("b", 0, 2), ("gr", 1, 1), ("t2",), ("d", 1, 0), ("c", 0, 1), ("gr", 1, 2),
+    ("gl", 0), ("c", 0, 2), ("a", 0, 3), ("e", 1, 0), ("p", 1, 0), ("d", 0, 1), ("gl", 1),
+    ("d", 0, 2), ("b", 0, 3), ("a", 1, 3), ("a", 1, 2), ("e", 0, 1), ("d", 0, 4), ("c", 0, 3),
+    ("e", 0, 2), ("f", 0, 1), ("b", 1, 3), ("f", 1, 0), ("f", 0, 2), ("d", 0, 3), ("b", 1, 2),
+    ("a", 1, 1), ("fo", 0), ("e", 0, 4), ("c", 1, 3), ("e", 0, 3), ("b", 1, 1), ("f", 0, 3),
+    ("d", 1, 3), ("c", 1, 2), ("c", 1, 1), ("e", 1, 3), ("p", 1, 3), ("f", 1, 3), ("fo", 3),
+    ("d", 1, 2), ("b", 1, 4), ("e", 1, 1), ("e", 1, 2), ("f1s", 1, 2), ("fo", 1), ("f", 1, 1),
+    ("f", 1, 2), ("d", 0, 0), ("f", 0, 4), ("c", 1, 4), ("fp", 0), ("e", 0, 0), ("fp", 3),
+    ("f1s", 1, 4), ("f", 0, 0), ("g", 0, 4), ("sg", 0), ("g", 0, 0), ("f1s", 1, 1),
+    ("e", 1, 4), ("fo", 4), ("f1r", 1, 2), ("fp", 4), ("f", 1, 4), ("g", 1, 4), ("fo", 2),
+    ("h", 0), ("g", 1, 0), ("sg", 1), ("fp", 1), ("fp", 2), ("h", 1),
 )
 
 

time: 109 us -> 109 us (level)
  no operation moved by 1% of the time
where the time goes in v5:
time: 109 us
  Pallas kernels  108 us (99%)
    pallas_call x1, Pallas kernels, local(): pl.pallas_call(kernel, out_shape=(pltpu.VMEM((B, W), BF), pltpu.VMEM((B,...  103 us
    pallas_call x1, Pallas kernels, local(): pl.pallas_call(widen, out_shape=(jax.ShapeDtypeStruct((B, W), BF), jax.Sh...  5.53 us

profile of v5, /device:TPU:1, one launch (start us, length us, event | category | flops | bytes accessed | tf_op | source)
XLA Modules:
  0.0 109.1 jit_solution(12362067862124929276)
XLA Ops:
  0.6 102.8 %ffn.1 = (bf16[32,1792]{1,0:T(8,128)(2,1)S(1)}, bf16[32,1792]{1,0:T(8,128)(2,1)S(1)}, bf16[896,1792]{1,0:T(8,128)(2,1)S(1)}, bf16[896,1792]{1,0:T(8,128)(2,1)S(1)}) custom-call(bf16[32,1792]{1,0:T(8,128)(2,1)} %tok_ref.1, bf16[1792,1792]{1,0:T(8,128)(2,1)} %w1_ref.1, bf16[1792,1792]{1,0:T(8,128)(2,1)} %w2_ref.1, bf16[32,1792]{1,0:T(8,128)(2,1)} %up_ref.1), custom_call_target="tpu_custom_call" | custom-call | flops 19730006016 | bytes 16777216 | tf_op jit(solution)/shard_map/ffn/pallas_call | solution.py:474
  103.4 5.5 %widen.1 = (bf16[32,1792]{1,0:T(8,128)(2,1)}, bf16[32,1792]{1,0:T(8,128)(2,1)}, f32[896,1792]{1,0:T(8,128)}, f32[896,1792]{1,0:T(8,128)}) custom-call(bf16[32,1792]{1,0:T(8,128)(2,1)S(1)} %get-tuple-element.8.lo_in, bf16[32,1792]{1,0:T(8,128)(2,1)S(1)} %get-tuple-element.9.tg_in, bf16[896,1792]{1,0:T(8,128)(2,1)S(1)} %get-tuple-element.10.fg_in, ...), custom_call_target="tpu_custom_call" | custom-call | tf_op jit(solution)/shard_map/widen/pallas_call | solution.py:517
